TPU v7x, 128 devices: a whole 4x4x4 slice. The times are simulated.
128 devices in a mesh: prompt: 4 (over y), resp: 32 (over z, x, core).
Axes of the slice: x: 4, y: 4, z: 4, core: 2. Of those that a mesh axis runs over, the one named last changes fastest.
Arguments:
- prompt_rows: bfloat16 [2048, 5120], P(('prompt', 'resp')), may hold values from -6 to 6
- key_weight: bfloat16 [5120, 512], replicated, may hold values from -0.078125 to 0.078125
- value_weight: bfloat16 [5120, 512], replicated, may hold values from -0.078125 to 0.078125
- queries: bfloat16 [16384, 2560], P(('prompt', 'resp')), may hold values from -180 to 180
- own_keys: bfloat16 [16384, 512], P(('prompt', 'resp')), may hold values from -6 to 6
- own_values: bfloat16 [16384, 512], P(('prompt', 'resp')), may hold values from -6 to 6
- out_grad: bfloat16 [16384, 2560], P(('prompt', 'resp')), may hold values from -24 to 24
- first_length: int32 [128], P(('prompt', 'resp')), may hold values from 16 to 112
- resp_prompt: int32 [128, 2], P(('prompt', 'resp')), may hold values from 0 to 3
Outputs:
- query_grad: bfloat16 [16384, 2560], P(('prompt', 'resp'))
- key_grad: bfloat16 [16384, 512], P(('prompt', 'resp'))
- value_grad: bfloat16 [16384, 512], P(('prompt', 'resp'))
- prompt_grad: bfloat16 [2048, 5120], P(('prompt', 'resp'))
All inputs are finite; a program needn't handle non-finite values.
Results may differ from a plain program's by a relative error of at most 0.038.
Values may be sent and summed in bfloat16 or wider, within the bound.
A program may use at most 192 MiB of HBM per device.

v0:
```python
import jax
import jax.numpy as jnp
from jax import lax
from jax.sharding import PartitionSpec as P

E = 128
PLEN = 512


def block_scores(query_heads, key_block):
    keys = key_block.reshape(key_block.shape[0], query_heads.shape[1], E)
    return jnp.einsum(
        "rkge,jke->kgrj", query_heads, keys, preferred_element_type=jnp.float32
    ) * E ** (-0.5)


def value_products(grad_heads, value_block):
    values = value_block.reshape(value_block.shape[0], grad_heads.shape[1], E)
    return jnp.einsum("rkge,jke->kgrj", grad_heads, values, preferred_element_type=jnp.float32)


def attend(query_heads, grad_heads, blocks):
    row_max = None
    row_total = None
    for key_block, value_block, visible in blocks:
        scores = jnp.where(visible, block_scores(query_heads, key_block), -jnp.inf)
        block_max = jnp.max(scores, axis=-1)
        if row_max is None:
            row_max = block_max
            row_total = jnp.sum(jnp.exp(scores - row_max[..., None]), axis=-1)
        else:
            new_max = jnp.maximum(row_max, block_max)
            row_total = row_total * jnp.exp(row_max - new_max) + jnp.sum(
                jnp.exp(scores - new_max[..., None]), axis=-1
            )
            row_max = new_max

    def probabilities(key_block, visible):
        scores = block_scores(query_heads, key_block)
        return jnp.where(visible, jnp.exp(scores - row_max[..., None]) / row_total[..., None], 0.0)

    delta = jnp.zeros_like(row_max)
    for key_block, value_block, visible in blocks:
        probs_low = probabilities(key_block, visible).astype(jnp.bfloat16)
        delta = delta + jnp.sum(
            probs_low.astype(jnp.float32) * value_products(grad_heads, value_block), axis=-1
        )
    query_sum = jnp.zeros(query_heads.shape, jnp.float32)
    block_grads = []
    for key_block, value_block, visible in blocks:
        probs = probabilities(key_block, visible)
        probs_low = probs.astype(jnp.bfloat16)
        dscores = (probs * (value_products(grad_heads, value_block) - delta[..., None])).astype(
            jnp.bfloat16
        )
        keys = key_block.reshape(key_block.shape[0], query_heads.shape[1], E)
        query_sum = query_sum + jnp.einsum(
            "kgrj,jke->rkge", dscores, keys, preferred_element_type=jnp.float32
        )
        key_part = jnp.einsum(
            "kgrj,rkge->jke", dscores, query_heads, preferred_element_type=jnp.float32
        ) * E ** (-0.5)
        value_part = jnp.einsum(
            "kgrj,rkge->jke", probs_low, grad_heads, preferred_element_type=jnp.float32
        )
        block_grads.append(
            (key_part.reshape(key_block.shape[0], -1), value_part.reshape(key_block.shape[0], -1))
        )
    return (query_sum * E ** (-0.5), block_grads)


def per_device(
    prompt_rows,
    key_weight,
    value_weight,
    queries,
    own_keys,
    own_values,
    out_grad,
    first_length,
    resp_prompt,
):
    prefix_keys = jnp.dot(prompt_rows, key_weight, preferred_element_type=jnp.float32).astype(
        jnp.bfloat16
    )
    prefix_values = jnp.dot(prompt_rows, value_weight, preferred_element_type=jnp.float32).astype(
        jnp.bfloat16
    )
    all_keys, all_values = (
        lax.all_gather(prefix_keys, ("prompt", "resp"), axis=0, tiled=True),
        lax.all_gather(prefix_values, ("prompt", "resp"), axis=0, tiled=True),
    )
    kv_count = own_keys.shape[1] // E
    head_count = queries.shape[1] // E
    row_count = queries.shape[0]
    query_heads = queries.reshape(row_count, kv_count, head_count // kv_count, E)
    grad_heads = out_grad.reshape(row_count, kv_count, head_count // kv_count, E)
    position = jnp.arange(row_count, dtype=jnp.int32)
    boundary = first_length[0]
    second = position >= boundary
    own_mask = (second[:, None] == second[None, :]) & (position[None, :] <= position[:, None])
    prompt_pair = resp_prompt[0]
    blocks = [(own_keys, own_values, own_mask)]
    row_prompt = jnp.where(second, prompt_pair[1], prompt_pair[0])
    for prompt in range(all_keys.shape[0] // PLEN):
        seen = jnp.broadcast_to((row_prompt == prompt)[:, None], (row_count, PLEN))
        blocks.append(
            (
                all_keys[prompt * PLEN : (prompt + 1) * PLEN],
                all_values[prompt * PLEN : (prompt + 1) * PLEN],
                seen,
            )
        )
    query_sum, block_grads = attend(query_heads, grad_heads, blocks)
    key_total = jnp.concatenate([grads[0] for grads in block_grads[1:]], axis=0)
    value_total = jnp.concatenate([grads[1] for grads in block_grads[1:]], axis=0)
    key_share, value_share = (
        lax.psum_scatter(key_total, ("prompt", "resp"), scatter_dimension=0, tiled=True),
        lax.psum_scatter(value_total, ("prompt", "resp"), scatter_dimension=0, tiled=True),
    )
    contract = (((1,), (1,)), ((), ()))
    prompt_grad = lax.dot_general(
        key_share.astype(jnp.bfloat16), key_weight, contract, preferred_element_type=jnp.float32
    )
    prompt_grad = prompt_grad + lax.dot_general(
        value_share.astype(jnp.bfloat16), value_weight, contract, preferred_element_type=jnp.float32
    )
    query_grad = query_sum.reshape(row_count, -1).astype(jnp.bfloat16)
    key_grad = block_grads[0][0].astype(jnp.bfloat16)
    value_grad = block_grads[0][1].astype(jnp.bfloat16)
    return (query_grad, key_grad, value_grad, prompt_grad.astype(jnp.bfloat16))


def solution(mesh):
    return jax.shard_map(
        per_device,
        mesh=mesh,
        in_specs=(
            P(("prompt", "resp"), None),
            P(),
            P(),
            P(("prompt", "resp"), None),
            P(("prompt", "resp"), None),
            P(("prompt", "resp"), None),
            P(("prompt", "resp"), None),
            P(("prompt", "resp")),
            P(("prompt", "resp"), None),
        ),
        out_specs=(
            P(("prompt", "resp"), None),
            P(("prompt", "resp"), None),
            P(("prompt", "resp"), None),
            P(("prompt", "resp"), None),
        ),
        check_vma=False,
    )
```

profile of v0, /device:TPU:1, one launch (start us, length us, event | category | flops | bytes accessed | tf_op | source)
XLA Modules:
  0.0 1520.9 jit_solution(16129165563088995668)
XLA Ops:
  8.1 3.9 convolution_convert_fusion
  12.0 3.9 convolution_convert_fusion.1
  19.0 1.2 broadcast_compare_fusion
  20.7 1.1 copy-done.11
  22.0 59.1 %all-gather.5.cloned.1.call-done = bf16[2048,512]{1,0:T(8,128)(2,1)} async-done(((bf16[16,512]{1,0:T(8,128)(2,1)}), bf16[2048,512]{1,0:T(8,128)(2,1)}) %all-gather.5.cloned.1.call-update) | async-done | bytes 2097168 | tf_op jit(solution)/shard_map/all_gather | solution.py:91
  81.1 2.7 fusion.70
  84.7 62.9 %all-gather.3.cloned.1.call-done = bf16[2048,512]{1,0:T(8,128)(2,1)} async-done(((bf16[16,512]{1,0:T(8,128)(2,1)}), bf16[2048,512]{1,0:T(8,128)(2,1)}) %all-gather.3.cloned.1.call-update) | async-done | bytes 2097168 | tf_op jit(solution)/shard_map/all_gather | solution.py:90
  147.6 2.7 fusion.71
  150.8 1.4 reshape.207
  152.5 2.2 reshape.206
  154.7 1.3 copy.182
  156.0 2.2 reshape.205
  158.2 2.1 copy.180
  160.3 2.0 reshape.213
  162.2 2.0 reshape.211
  164.2 2.0 reshape.210
  166.2 4.3 fusion.51
  170.5 3.2 fusion.53
  173.7 3.1 fusion.55
  180.6 1.0 exponential_reduce_fusion.1
  181.7 1.0 exponential_reduce_fusion.2
  182.7 1.2 exponential_reduce_fusion.3
  184.0 1.0 exponential_reduce_fusion
  185.1 1.5 multiply_reduce_fusion
  186.6 12.8 fusion.10
  199.4 19.1 %fusion.12 = (bf16[4,5,128,512]{2,3,1,0:T(8,128)(2,1)}, bf16[4,5,128,512]{2,3,1,0:T(8,128)(2,1)}, bf16[4,5,128,512]{2,3,1,0:T(8,128)(2,1)}, bf16[4,5,128,512]{2,3,1,0:T(8,128)(2,1)S(1)}) fusion(f32[4,512,128,5]{2,1,3,0:T(8,128)} %get-tuple-element.53, f32[4,5,128]{2,1,0:T(8,128)S(1)} %add_add_fusion, f32[4,5,128]{2,1,0:T(8,128)S(1)} %multiply_add_fusion, ...), kind=kLoop, calls=%fused_computation.21 | loop fusion | flops 36700160 | bytes 52460032 | tf_op jit(solution)/shard_map/convert_element_type | solution.py:53
  218.5 2.8 fusion.36
  221.4 2.7 fusion.37
  226.0 2.3 pad_maximum_fusion
  228.4 5.4 copy.236
  234.1 4.1 fusion.46
  238.2 4.0 fusion.44
  242.2 1.3 fusion.40
  243.5 1.3 fusion.42
  244.8 2.4 pad_maximum_fusion.1
  247.2 5.4 copy.238
  252.6 2.5 fusion.49
  255.1 1.7 copy.155
  256.8 2.1 multiply_convert_fusion
  258.9 1.0 fusion.50
  260.0 1.7 copy.154
  261.6 2.6 convolution_bitcast_fusion.4
  264.3 1.7 convolution_bitcast_fusion.3
  267.8 1.1 copy.153
  268.8 599.6 %reduce-scatter.7.cloned.1.call-done = f32[16,512]{1,0:T(8,128)} async-done(((f32[2048,512]{1,0:T(8,128)}), f32[16,512]{1,0:T(8,128)}) %reduce-scatter.7.cloned.1.call-update) | async-done | bytes 32784
  869.4 3.9 fusion.73
  873.3 635.5 %reduce-scatter.9.cloned.1.call-done = f32[16,512]{1,0:T(8,128)} async-done(((f32[2048,512]{1,0:T(8,128)}), f32[16,512]{1,0:T(8,128)}) %reduce-scatter.9.cloned.1.call-update) | async-done | bytes 32784
  1509.7 4.6 fusion
  (105 shorter events, 15.4 us)
Async XLA Ops:
  7.2 0.9 copy-start
  7.2 9.5 copy-start.26
  7.2 9.7 copy-start.27
  7.2 10.3 copy-start.23
  7.2 10.7 copy-start.24
  7.2 73.9 %all-gather.5.cloned.1.call-start = ((), (), s32[]{:S(2)}) async-start(), calls=%async_computation.3 | async-start | bytes 2113536 | tf_op jit(solution)/shard_map/all_gather | solution.py:91
  12.0 6.2 copy-start.29
  12.0 135.6 %all-gather.3.cloned.1.call-start = ((), (), s32[]{:S(2)}) async-start(), calls=%async_computation.2 | async-start | bytes 2113536 | tf_op jit(solution)/shard_map/all_gather | solution.py:90
  16.0 852.5 %reduce-scatter.7.cloned.1.call-start = ((), (), s32[]{:S(2)}) async-start(), calls=%async_computation.4 | async-start | bytes 4227072
  18.2 168.4 %copy-start.9 = (bf16[128,2560]{0,1:T(8,128)(2,1)}, bf16[128,2560]{0,1:T(8,128)(2,1)S(1)}, u32[]{:S(2)}) copy-start(bf16[128,2560]{0,1:T(8,128)(2,1)S(1)} %copy.122) | copy-start | bytes 1966084
  20.7 1.1 copy-start.11
  150.8 26.0 %copy-start.15 = (bf16[512,4,128,1]{0,2,3,1:T(8,128)(2,1)}, bf16[512,4,128,1]{0,2,3,1:T(8,128)(2,1)S(1)}, u32[]{:S(2)}) copy-start(bf16[512,4,128,1]{0,2,3,1:T(8,128)(2,1)S(1)} %copy.178) | copy-start | bytes 1572868
  152.5 27.2 %copy-start.13 = (bf16[512,4,128,1]{0,2,3,1:T(8,128)(2,1)}, bf16[512,4,128,1]{0,2,3,1:T(8,128)(2,1)S(1)}, u32[]{:S(2)}) copy-start(bf16[512,4,128,1]{0,2,3,1:T(8,128)(2,1)S(1)} %copy.184) | copy-start | bytes 1572868
  156.0 22.8 %copy-start.16 = (bf16[512,4,128,1]{0,2,3,1:T(8,128)(2,1)}, bf16[512,4,128,1]{0,2,3,1:T(8,128)(2,1)S(1)}, u32[]{:S(2)}) copy-start(bf16[512,4,128,1]{0,2,3,1:T(8,128)(2,1)S(1)} %copy.182) | copy-start | bytes 1572868
  166.2 4.3 copy-start.21
  170.5 3.2 copy-start.22
  176.8 1.0 copy-start.18
  177.7 8.9 copy-start.3
  178.7 2.9 copy-start.4
  179.7 6.9 copy-start.2
  180.6 3.4 copy-start.5
  182.7 2.4 copy-start.12
  182.7 2.4 copy-start.28
  184.0 2.6 copy-start.25
  218.5 5.5 copy-start.6
  233.8 1275.0 %reduce-scatter.9.cloned.1.call-start = ((), (), s32[]{:S(2)}) async-start(), calls=%async_computation.5 | async-start | bytes 4227072
  234.1 4.1 copy-start.10
  234.1 8.1 slice-start.2
  238.2 4.0 slice-start.3
  238.2 5.3 slice-start
  242.2 1.3 slice-start.1
  258.9 1.1 copy-start.19
  261.6 2.7 copy-start.8
  261.6 4.4 copy-start.7
  261.6 4.4 copy-start.17
  264.3 2.3 copy-start.14
  266.0 1.2 copy-start.20
  868.5 645.9 %copy-start.1 = (bf16[16,5120]{1,0:T(8,128)(2,1)S(1)}, bf16[16,5120]{1,0:T(8,128)(2,1)}, u32[]{:S(2)}) copy-start(bf16[16,5120]{1,0:T(8,128)(2,1)} %param.9) | copy-start | bytes 491524
Sparse Core Ops, SparseCore 0:
  12.1 68.9 all-gather.4
  84.8 62.7 all-gather.2
  233.9 634.5 reduce-scatter.6
  870.8 637.9 reduce-scatter.8
where the time goes:
time: 1530 us; the launch traced here: 1520 us
  waiting for transfers between devices  1360 us (89%)
  matrix products  72.9 us (5%)
  local copies, waits for them, and re-layouts  43.6 us (3%)
  other arithmetic  31.8 us (2%)
    unnamed x6, waiting for transfers between devices  1240 us
    all_gather x1, waiting for transfers between devices, per_device(): lax.all_gather(prefix_keys, ('prompt', 'resp'), axis=0, tiled=True)  62.9 us
    all_gather x1, waiting for transfers between devices, per_device(): lax.all_gather(prefix_values, ('prompt', 'resp'), axis=0, tiled=True)  59.1 us
  transfers between devices with their start and end apart: 4, of which 4 were waited for; matrix products, arithmetic and copies ran while one was open for 3% of the time, Pallas kernels for 0%

commit v1 on v0

v1 whole, which is shorter than its diff:
```python
import functools

import jax
import jax.numpy as jnp
from jax import lax
from jax.experimental import pallas as pl
from jax.experimental.pallas import tpu as pltpu
from jax.sharding import PartitionSpec as P

MESH = pl.DeviceIdType.MESH
E = 128
KVH = 4
G = 2
GROUP = 5
ROWS = 128
HALF = 16
SCALE = E ** (-0.5)
LOG2E = 1.4426950408889634
ORDERS = ((0, 1, 2), (1, 2, 0), (2, 0, 1))
ORDER_OF = (((0, 1), (2, 0)), ((1, 2), (0, 2)))


def kernel(
    dims,
    prompt_rows,
    key_weight,
    value_weight,
    queries,
    own_keys,
    own_values,
    out_grad,
    first_length,
    resp_prompt,
    query_grad,
    key_grad,
    value_grad,
    prompt_grad,
    wk,
    wv,
    rows,
    q_in,
    g_in,
    own_in,
    scal_out,
    scal_in,
    scal,
    kv_0,
    kv_1,
    keys_ab,
    values_ab,
    q_ab,
    g_ab,
    scores,
    dprobs,
    probs_t,
    dscores_t,
    parts,
    contrib,
    recv1,
    acc1,
    recv2,
    acc2,
    recv3,
    share,
    final,
    dq_out,
    own_out,
    w_sem,
    in_sem,
    x_send,
    x_recv,
    ag_send,
    ag_recv,
    rs_send,
    rs_recv,
    out_sem,
):
    kv = (kv_0, kv_1)
    ny, nz, nx = dims
    prompts = ny
    plen = nz * nx * 2 * HALF
    depth = key_weight.shape[0]
    kcols = G * E
    qcols = G * GROUP * E
    p_index = lax.axis_index("prompt")
    r_index = lax.axis_index("resp")
    core = lax.rem(r_index, 2)
    chip = lax.div(r_index, 2)
    me = (p_index, lax.div(chip, nx), lax.rem(chip, nx))
    other = 1 - core

    def device(coords, on_core):
        return (coords[0], (coords[1] * nx + coords[2]) * 2 + on_core)

    def shifted(dim, off):
        return lax.rem(me[dim] + off, dims[dim])

    def peer(dim, off):
        coords = list(me)
        coords[dim] = shifted(dim, off)
        return device(coords, core)

    partner = device(me, other)

    steps = 5
    piece = depth // steps
    mine_k = pl.ds(pl.multiple_of(core * kcols, kcols), kcols)
    theirs_k = pl.ds(pl.multiple_of(other * kcols, kcols), kcols)
    mine_q = pl.ds(pl.multiple_of(core * qcols, E), qcols)
    theirs_q = pl.ds(pl.multiple_of(other * qcols, E), qcols)
    my_half = pl.ds(pl.multiple_of(core * HALF, HALF), HALF)

    rows_copy = pltpu.make_async_copy(prompt_rows, rows.at[my_half], in_sem.at[0])
    rows_copy.start()
    w_copies = []
    for s in range(steps):
        at = pl.ds(s * piece, piece)
        pair = (
            pltpu.make_async_copy(key_weight.at[at, mine_k], wk.at[at, mine_k], w_sem.at[0, s]),
            pltpu.make_async_copy(value_weight.at[at, mine_k], wv.at[at, mine_k], w_sem.at[1, s]),
        )
        for c in pair:
            c.start()
        w_copies.append(pair)

    barrier = pltpu.get_barrier_semaphore()
    pl.semaphore_signal(barrier, inc=1, device_id=partner, device_id_type=MESH)
    count = 1
    for dim in range(3):
        for off in range(1, dims[dim]):
            pl.semaphore_signal(barrier, inc=1, device_id=peer(dim, off), device_id_type=MESH)
            count += 1
    pl.semaphore_wait(barrier, count)

    def swap(src, dst, index):
        c = pltpu.make_async_remote_copy(
            src_ref=src, dst_ref=dst, send_sem=x_send.at[index], recv_sem=x_recv.at[index],
            device_id=partner, device_id_type=MESH,
        )
        c.start()
        return c

    rows_swap = swap(prompt_rows, rows.at[my_half], 0)
    lane8 = lax.broadcasted_iota(jnp.int32, (8, 128), 1)
    l_mine = first_length[0]
    a_mine = resp_prompt[0, 0]
    b_mine = resp_prompt[0, 1]
    scal_out[...] = jnp.where(lane8 == 0, l_mine, jnp.where(lane8 == 1, a_mine, b_mine))
    scal_swap = swap(scal_out, scal_in, 1)
    own_swaps = [
        swap(own_keys.at[:, theirs_k], own_in.at[1, 0], 2),
        swap(own_values.at[:, theirs_k], own_in.at[1, 1], 3),
    ]
    q_swap = swap(queries.at[:, theirs_q], q_in.at[1], 4)
    g_swap = swap(out_grad.at[:, theirs_q], g_in.at[1], 5)
    local = [
        pltpu.make_async_copy(own_keys.at[:, mine_k], own_in.at[0, 0], in_sem.at[1]),
        pltpu.make_async_copy(own_values.at[:, mine_k], own_in.at[0, 1], in_sem.at[2]),
        pltpu.make_async_copy(queries.at[:, mine_q], q_in.at[0], in_sem.at[3]),
        pltpu.make_async_copy(out_grad.at[:, mine_q], g_in.at[0], in_sem.at[4]),
    ]
    for c in local:
        c.start()

    rows_copy.wait()
    rows_swap.wait_recv()
    k_proj = jnp.zeros((2 * HALF, kcols), jnp.float32)
    v_proj = jnp.zeros((2 * HALF, kcols), jnp.float32)
    for s in range(steps):
        at = pl.ds(s * piece, piece)
        x = rows[:, at]
        w_copies[s][0].wait()
        k_proj = k_proj + jnp.dot(x, wk[at, mine_k], preferred_element_type=jnp.float32)
        w_copies[s][1].wait()
        v_proj = v_proj + jnp.dot(x, wv[at, mine_k], preferred_element_type=jnp.float32)
    k_proj = k_proj.astype(jnp.bfloat16)
    v_proj = v_proj.astype(jnp.bfloat16)
    for g in range(G):
        for h in range(2):
            at = (slice(h * HALF, (h + 1) * HALF), slice(g * E, (g + 1) * E))
            kv[g][0, h, me[0], me[1], me[2]] = k_proj[at]
            kv[g][1, h, me[0], me[1], me[2]] = v_proj[at]

    pieces = [(g, t, h) for g in range(G) for t in range(2) for h in range(2)]

    def gather_copies(g, t, h, phase):
        order = ORDERS[ORDER_OF[g][t][h]]
        index = [me[0], me[1], me[2]]
        for d in order[:phase]:
            index[d] = slice(None)
        block = kv[g].at[t, h, index[0], index[1], index[2]]
        number = (g * 2 + t) * 2 + h
        return [
            pltpu.make_async_remote_copy(
                src_ref=block, dst_ref=block,
                send_sem=ag_send.at[number, phase, off - 1], recv_sem=ag_recv.at[number, phase, off - 1],
                device_id=peer(order[phase], off), device_id_type=MESH,
            )
            for off in range(1, dims[order[phase]])
        ]

    sends = []
    gathers = {}

    def gather_start(name, phase):
        gathers[name, phase] = gather_copies(*name, phase)
        for c in gathers[name, phase]:
            c.start()
        sends.extend(gathers[name, phase])

    def gather_wait(name, phase):
        for c in gathers[name, phase]:
            c.wait_recv()

    for name in pieces:
        gather_start(name, 0)
    for phase in range(2):
        for name in pieces:
            gather_wait(name, phase)
            gather_start(name, phase + 1)

    late = [
        pltpu.make_async_copy(key_weight.at[:, theirs_k], wk.at[:, theirs_k], w_sem.at[0, steps]),
        pltpu.make_async_copy(value_weight.at[:, theirs_k], wv.at[:, theirs_k], w_sem.at[1, steps]),
    ]
    for c in late:
        c.start()

    scal_swap.wait_recv()
    to_smem = pltpu.make_async_copy(scal_in, scal, in_sem.at[5])
    to_smem.start()
    to_smem.wait()
    first = (l_mine, scal[0, 0])
    prompt_a = (a_mine, scal[0, 1])
    prompt_b = (b_mine, scal[0, 2])
    for c in local:
        c.wait()
    for c in own_swaps:
        c.wait_recv()
    q_swap.wait_recv()
    g_swap.wait_recv()

    sub_j = lax.broadcasted_iota(jnp.int32, (ROWS, E), 0)
    lane_i = lax.broadcasted_iota(jnp.int32, (ROWS, E), 1)
    lane_1 = lax.broadcasted_iota(jnp.int32, (1, E), 1)
    wide = GROUP * E
    total_keys = plen + ROWS

    def attend(g, d):
        boundary = first[d]
        in_a = jnp.where(sub_j < boundary, 1.0, 0.0).astype(jnp.bfloat16)
        in_b = jnp.where(sub_j < boundary, 0.0, 1.0).astype(jnp.bfloat16)
        head_k = slice(g * E, (g + 1) * E)
        for t, dst in ((0, keys_ab), (1, values_ab)):
            for which, prompt in ((0, prompt_a[d]), (1, prompt_b[d])):
                cols = slice(which * E, (which + 1) * E)
                for h in range(2):
                    block = kv[g][t, h, prompt]
                    dst[h * (plen // 2) : (h + 1) * (plen // 2), cols] = block.reshape(plen // 2, E)
                dst[plen:, cols] = own_in[d, t, :, head_k]
        for h in range(GROUP):
            cols = slice((g * GROUP + h) * E, (g * GROUP + h + 1) * E)
            at = slice(h * E, (h + 1) * E)
            q = q_in[d, :, cols]
            q_ab[at, 0:E] = q * in_a
            q_ab[at, E:] = q * in_b
            o = g_in[d, :, cols]
            g_ab[at, 0:E] = o * in_a
            g_ab[at, E:] = o * in_b
        both = (((1,), (1,)), ((), ()))
        scores[...] = lax.dot_general(keys_ab[...], q_ab[...], both, preferred_element_type=jnp.float32)
        dprobs[...] = lax.dot_general(values_ab[...], g_ab[...], both, preferred_element_type=jnp.float32)
        seen = (sub_j <= lane_i) & ((sub_j < boundary) == (lane_i < boundary))
        for h in range(GROUP):
            at = slice(h * E, (h + 1) * E)
            s_pre = scores[:plen, at]
            s_own = jnp.where(seen, scores[plen:, at], -jnp.inf)
            top = jnp.maximum(jnp.max(s_pre, axis=0, keepdims=True), jnp.max(s_own, axis=0, keepdims=True))
            e_pre = jnp.exp2((s_pre - top) * (SCALE * LOG2E))
            e_own = jnp.exp2((s_own - top) * (SCALE * LOG2E))
            total = jnp.sum(e_pre, axis=0, keepdims=True) + jnp.sum(e_own, axis=0, keepdims=True)
            inverse = 1.0 / total
            p_pre = e_pre * inverse
            p_own = e_own * inverse
            low_pre = p_pre.astype(jnp.bfloat16)
            low_own = p_own.astype(jnp.bfloat16)
            probs_t[:plen, at] = low_pre
            probs_t[plen:, at] = low_own
            dp_pre = dprobs[:plen, at]
            dp_own = dprobs[plen:, at]
            delta = jnp.sum(low_pre.astype(jnp.float32) * dp_pre, axis=0, keepdims=True) + jnp.sum(
                low_own.astype(jnp.float32) * dp_own, axis=0, keepdims=True
            )
            dscores_t[:plen, at] = (p_pre * (dp_pre - delta)).astype(jnp.bfloat16)
            dscores_t[plen:, at] = (p_own * (dp_own - delta)).astype(jnp.bfloat16)
        parts[d, 1] = jnp.dot(probs_t[...], g_ab[...], preferred_element_type=jnp.float32)
        parts[d, 0] = jnp.dot(dscores_t[...], q_ab[...], preferred_element_type=jnp.float32)
        dq_t = jnp.dot(keys_ab[...].T, dscores_t[...], preferred_element_type=jnp.float32)
        for h in range(GROUP):
            at = slice(h * E, (h + 1) * E)
            picked = jnp.where(lane_1 < boundary, dq_t[:E, at], dq_t[E:, at]) * SCALE
            cols = slice((g * GROUP + h) * E, (g * GROUP + h + 1) * E)
            dq_out[d, :, cols] = picked.T.astype(jnp.bfloat16)
        own_out[d, 0, :, head_k] = ((parts[d, 0, plen:, :E] + parts[d, 0, plen:, E:]) * SCALE).astype(jnp.bfloat16)
        own_out[d, 1, :, head_k] = (parts[d, 1, plen:, :E] + parts[d, 1, plen:, E:]).astype(jnp.bfloat16)

    def contribute(g):
        for t in range(2):
            unit = SCALE if t == 0 else 1.0
            for h in range(2):
                at = slice(h * (plen // 2), (h + 1) * (plen // 2))
                for p in range(prompts):
                    total = None
                    for d in range(2):
                        for which, prompt in ((0, prompt_a[d]), (1, prompt_b[d])):
                            gate = jnp.where(prompt == p, unit, 0.0).astype(jnp.float32)
                            term = parts[d, t, at, which * E : (which + 1) * E] * gate
                            total = term if total is None else total + term
                    contrib[g, t, h, p] = total.astype(jnp.bfloat16).reshape(nz, nx, HALF, E)

    def scatter_copies(g, t, h, phase):
        order = ORDERS[ORDER_OF[g][t][h]][::-1]
        dim = order[phase]
        number = (g * 2 + t) * 2 + h
        left = [d for d in range(3) if d not in order[:phase]]
        out = []
        for off in range(1, dims[dim]):
            index = tuple(shifted(d, off) if d == dim else slice(None) for d in left)
            if phase == 0:
                src, dst = contrib.at[(g, t, h) + index], recv1.at[g, t, h, off - 1]
            elif phase == 1:
                src, dst = acc1.at[(g, t, h) + index], recv2.at[g, t, h, off - 1]
            else:
                src, dst = acc2.at[(g, t, h) + index], recv3.at[g, t, h, off - 1]
            out.append(
                pltpu.make_async_remote_copy(
                    src_ref=src, dst_ref=dst,
                    send_sem=rs_send.at[number, phase, off - 1], recv_sem=rs_recv.at[number, phase, off - 1],
                    device_id=peer(dim, off), device_id_type=MESH,
                )
            )
        return out

    scatters = {}

    def scatter_start(name, phase):
        scatters[name, phase] = scatter_copies(*name, phase)
        for c in scatters[name, phase]:
            c.start()
        sends.extend(scatters[name, phase])

    def scatter_finish(name, phase):
        order = ORDERS[ORDER_OF[name[0]][name[1]][name[2]]][::-1]
        dim = order[phase]
        left = [d for d in range(3) if d not in order[:phase]]
        for c in scatters[name, phase]:
            c.wait_recv()
        index = tuple(me[d] if d == dim else slice(None) for d in left)
        source, arrived = ((contrib, recv1), (acc1, recv2), (acc2, recv3))[phase]
        total = source[name + index].astype(jnp.float32)
        for off in range(1, dims[dim]):
            total = total + arrived[name + (off - 1,)].astype(jnp.float32)
        if phase < 2:
            (acc1, acc2)[phase][name] = total.astype(jnp.bfloat16)
        else:
            g, t, h = name
            share[h, :, (t * G + g) * E : (t * G + g + 1) * E] = total.astype(jnp.bfloat16)

    def of_head(g):
        return [name for name in pieces if name[0] == g]

    for name in of_head(0):
        gather_wait(name, 2)
    attend(0, 0)
    attend(0, 1)
    contribute(0)
    for name in of_head(0):
        scatter_start(name, 0)
    for name in of_head(1):
        gather_wait(name, 2)
    attend(1, 0)
    for name in of_head(0):
        scatter_finish(name, 0)
        scatter_start(name, 1)
    attend(1, 1)
    contribute(1)
    for name in of_head(1):
        scatter_start(name, 0)
    for name in of_head(0):
        scatter_finish(name, 1)
        scatter_start(name, 2)

    home = [
        pltpu.make_async_copy(dq_out.at[0], query_grad.at[:, mine_q], out_sem.at[0]),
        pltpu.make_async_copy(own_out.at[0, 0], key_grad.at[:, mine_k], out_sem.at[1]),
        pltpu.make_async_copy(own_out.at[0, 1], value_grad.at[:, mine_k], out_sem.at[2]),
    ]
    for c in home:
        c.start()
    away = [
        swap(dq_out.at[1], query_grad.at[:, mine_q], 6),
        swap(own_out.at[1, 0], key_grad.at[:, mine_k], 7),
        swap(own_out.at[1, 1], value_grad.at[:, mine_k], 8),
    ]

    for name in of_head(0):
        scatter_finish(name, 2)
    for phase in range(2):
        for name in of_head(1):
            scatter_finish(name, phase)
            scatter_start(name, phase + 1)
    for name in of_head(1):
        scatter_finish(name, 2)

    final_swap = swap(share.at[other], final.at[core], 9)
    final[core] = share[core]
    for c in late:
        c.wait()
    final_swap.wait_recv()
    x_k = jnp.concatenate([final[0, :, :kcols], final[1, :, :kcols]], axis=1)
    x_v = jnp.concatenate([final[0, :, kcols:], final[1, :, kcols:]], axis=1)
    tile = 512
    both = (((1,), (1,)), ((), ()))
    for n in range(depth // tile):
        at = slice(n * tile, (n + 1) * tile)
        total = lax.dot_general(x_k, wk[at, :], both, preferred_element_type=jnp.float32)
        total = total + lax.dot_general(x_v, wv[at, :], both, preferred_element_type=jnp.float32)
        prompt_grad[:, at] = total.astype(jnp.bfloat16)

    for c in sends:
        c.wait_send()
    for c in [rows_swap, scal_swap, q_swap, g_swap, final_swap] + own_swaps + away:
        c.wait_send()
    for c in home:
        c.wait()
    for c in away:
        c.wait_recv()


def per_device(dims, *arrays):
    ny, nz, nx = dims
    depth = arrays[0].shape[1]
    plen = nz * nx * 2 * HALF
    keys = plen + ROWS
    wide = GROUP * E
    bf16, f32 = jnp.bfloat16, jnp.float32
    most = max(dims) - 1
    assert ny == nz == nx
    n = nx
    vmem = pltpu.VMEM
    hbm = pl.BlockSpec(memory_space=pl.ANY)
    smem = pl.BlockSpec(memory_space=pltpu.SMEM)
    dma = pltpu.SemaphoreType.DMA
    scratch = [
        vmem((depth, KVH * E), bf16),
        vmem((depth, KVH * E), bf16),
        vmem((2 * HALF, depth), bf16),
        vmem((2, ROWS, G * wide), bf16),
        vmem((2, ROWS, G * wide), bf16),
        vmem((2, 2, ROWS, G * E), bf16),
        vmem((8, 128), jnp.int32),
        vmem((8, 128), jnp.int32),
        pltpu.SMEM((8, 128), jnp.int32),
        vmem((2, 2, n, n, n, HALF, E), bf16),
        vmem((2, 2, n, n, n, HALF, E), bf16),
        vmem((keys, 2 * E), bf16),
        vmem((keys, 2 * E), bf16),
        vmem((wide, 2 * E), bf16),
        vmem((wide, 2 * E), bf16),
        vmem((keys, wide), f32),
        vmem((keys, wide), f32),
        vmem((keys, wide), bf16),
        vmem((keys, wide), bf16),
        vmem((2, 2, keys, 2 * E), f32),
        vmem((G, 2, 2, n, n, n, HALF, E), bf16),
        vmem((G, 2, 2, n - 1, n, n, HALF, E), bf16),
        vmem((G, 2, 2, n, n, HALF, E), bf16),
        vmem((G, 2, 2, n - 1, n, HALF, E), bf16),
        vmem((G, 2, 2, n, HALF, E), bf16),
        vmem((G, 2, 2, n - 1, HALF, E), bf16),
        vmem((2, HALF, 2 * G * E), bf16),
        vmem((2, HALF, 2 * G * E), bf16),
        vmem((2, ROWS, G * wide), bf16),
        vmem((2, 2, ROWS, G * E), bf16),
        dma((2, 6)),
        dma((6,)),
        dma((10,)),
        dma((10,)),
        dma((8, 3, most)),
        dma((8, 3, most)),
        dma((8, 3, most)),
        dma((8, 3, most)),
        dma((3,)),
    ]
    shape = jax.ShapeDtypeStruct
    return pl.pallas_call(
        functools.partial(kernel, dims),
        out_shape=(
            shape((ROWS, KVH * wide), bf16),
            shape((ROWS, KVH * E), bf16),
            shape((ROWS, KVH * E), bf16),
            shape((HALF, depth), bf16),
        ),
        in_specs=[hbm] * 7 + [smem] * 2,
        out_specs=(hbm, hbm, hbm, pl.BlockSpec(memory_space=pltpu.VMEM)),
        scratch_shapes=scratch,
        compiler_params=pltpu.CompilerParams(
            collective_id=0, has_side_effects=True, vmem_limit_bytes=56 * 1024 * 1024
        ),
    )(*arrays)


def solution(mesh):
    ny = mesh.shape["prompt"]
    chips = mesh.shape["resp"] // 2
    nx = round(chips**0.5)
    dims = (ny, chips // nx, nx)
    rows = P(("prompt", "resp"), None)
    return jax.shard_map(
        functools.partial(per_device, dims),
        mesh=mesh,
        in_specs=(rows, P(), P(), rows, rows, rows, rows, P(("prompt", "resp")), rows),
        out_specs=(rows, rows, rows, rows),
        check_vma=False,
    )
```

time: 1530 us -> 71.6 us (0.05)
  waiting for transfers between devices: 1360 us -> 0 us
  matrix products: 72.9 us -> 0 us
  Pallas kernels: 0 us -> 63.4 us
  local copies, waits for them, and re-layouts: 43.6 us -> 6.69 us
  other arithmetic: 31.8 us -> 0 us
    unnamed x6 -> x0, waiting for transfers between devices: 1240 us -> none
    all_gather x2 -> x0, waiting for transfers between devices: 122 us -> none  [the longest x1 62.9 us: per_device(): lax.all_gather(prefix_keys, ('prompt', 'resp'), axis=0, tiled=True)]
    dot_general x29 -> x0, matrix products: 72.9 us -> none  [the longest x5 24.9 us: value_products(): jnp.einsum('rkge,jke->kgrj', grad_heads, values, preferred_element_type=j...]
    pallas_call x0 -> x1, Pallas kernels: none -> 63.4 us  [per_device(): pl.pallas_call(functools.partial(kernel, dims), out_shape=(shape((ROWS, K...]
    convert_element_type x2 -> x0, other arithmetic: 21.2 us -> none  [attend(): (probs * (value_products(grad_heads, value_block) - delta[..., None])).as...]
    reshape x15 -> x0, local copies, waits for them, and re-layouts: 17.5 us -> none  [the longest x8 9.85 us: block_scores(): keys = key_block.reshape(key_block.shape[0], query_heads.shape[1], E)]
  transfers between devices with their start and end apart: 4 -> 0, of which waited for: 4 -> 0; matrix products, arithmetic and copies ran while one was open for 3% -> 0% of each run, Pallas kernels for 0% -> 0%
where the time goes in v1:
time: 71.6 us; the launch traced here: 71.4 us
  Pallas kernels  63.4 us (89%)
  local copies, waits for them, and re-layouts  6.69 us (9%)
  between operations  1.29 us (2%)
    pallas_call x1, Pallas kernels, per_device(): pl.pallas_call(functools.partial(kernel, dims), out_shape=(shape((ROWS, K...  63.4 us
    unnamed x4, local copies, waits for them, and re-layouts  6.69 us

profile of v1, /device:TPU:1, one launch (start us, length us, event | category | flops | bytes accessed | tf_op | source)
XLA Modules:
  0.0 71.4 jit_solution(9923397569201008995)
XLA Ops:
  1.3 63.4 %shard_map.120 = (bf16[128,2560]{1,0:T(8,128)(2,1)}, bf16[128,512]{1,0:T(8,128)(2,1)}, bf16[128,512]{1,0:T(8,128)(2,1)}, bf16[16,5120]{1,0:T(8,128)(2,1)}) custom-call(bf16[16,5120]{1,0:T(8,128)(2,1)} %prompt_rows.1, bf16[5120,512]{1,0:T(8,128)(2,1)} %key_weight.1, bf16[5120,512]{1,0:T(8,128)(2,1)} %value_weight.1, bf16[128,2560]{1,0:T(8,128)(2,1)} %queries.1, ...), custom_call_target="tpu_custom_call" | custom-call | tf_op jit(solution)/shard_map/pallas_call | solution.py:496
  64.7 2.0 %copy.18 = bf16[128,2560]{1,0:T(8,128)(2,1)} copy(bf16[128,2560]{1,0:T(8,128)(2,1)} %get-tuple-element.8) | data formatting | bytes 1310720
  66.7 1.6 %copy.19 = bf16[128,512]{1,0:T(8,128)(2,1)} copy(bf16[128,512]{1,0:T(8,128)(2,1)} %get-tuple-element.9) | data formatting | bytes 262144
  68.3 1.6 %copy.20 = bf16[128,512]{1,0:T(8,128)(2,1)} copy(bf16[128,512]{1,0:T(8,128)(2,1)} %get-tuple-element.10) | data formatting | bytes 262144
  69.8 1.6 %copy.21 = bf16[16,5120]{1,0:T(8,128)(2,1)} copy(bf16[16,5120]{1,0:T(8,128)(2,1)} %get-tuple-element.11) | data formatting | bytes 327680

commit v2 on v1

--- a/solution.py
+++ b/solution.py
@@ -379,16 +379,13 @@
     for name in of_head(1):
         gather_wait(name, 2)
     attend(1, 0)
-    for name in of_head(0):
-        scatter_finish(name, 0)
-        scatter_start(name, 1)
     attend(1, 1)
     contribute(1)
     for name in of_head(1):
         scatter_start(name, 0)
     for name in of_head(0):
-        scatter_finish(name, 1)
-        scatter_start(name, 2)
+        scatter_finish(name, 0)
+        scatter_start(name, 1)
 
     home = [
         pltpu.make_async_copy(dq_out.at[0], query_grad.at[:, mine_q], out_sem.at[0]),
@@ -403,13 +400,13 @@
         swap(own_out.at[1, 1], value_grad.at[:, mine_k], 8),
     ]
 
-    for name in of_head(0):
-        scatter_finish(name, 2)
-    for phase in range(2):
-        for name in of_head(1):
-            scatter_finish(name, phase)
-            scatter_start(name, phase + 1)
     for name in of_head(1):
+        scatter_finish(name, 0)
+        scatter_start(name, 1)
+    for name in pieces:
+        scatter_finish(name, 1)
+        scatter_start(name, 2)
+    for name in pieces:
         scatter_finish(name, 2)
 
     final_swap = swap(share.at[other], final.at[core], 9)
@@ -435,6 +432,19 @@
         c.wait()
     for c in away:
         c.wait_recv()
+
+
+def hand_over(*refs):
+    sources, results, buffers, arrive, leave = refs[:4], refs[4:8], refs[8:12], refs[12], refs[13]
+    inward = [pltpu.make_async_copy(a, b, arrive.at[i]) for i, (a, b) in enumerate(zip(sources, buffers))]
+    outward = [pltpu.make_async_copy(b, c, leave.at[i]) for i, (b, c) in enumerate(zip(buffers, results))]
+    for c in inward:
+        c.start()
+    for c, after in zip(inward, outward):
+        c.wait()
+        after.start()
+    for c in outward:
+        c.wait()
 
 
 def per_device(dims, *arrays):
@@ -493,14 +503,15 @@
         dma((3,)),
     ]
     shape = jax.ShapeDtypeStruct
-    return pl.pallas_call(
+    results = (
+        shape((ROWS, KVH * wide), bf16),
+        shape((ROWS, KVH * E), bf16),
+        shape((ROWS, KVH * E), bf16),
+        shape((HALF, depth), bf16),
+    )
+    made = pl.pallas_call(
         functools.partial(kernel, dims),
-        out_shape=(
-            shape((ROWS, KVH * wide), bf16),
-            shape((ROWS, KVH * E), bf16),
-            shape((ROWS, KVH * E), bf16),
-            shape((HALF, depth), bf16),
-        ),
+        out_shape=results,
         in_specs=[hbm] * 7 + [smem] * 2,
         out_specs=(hbm, hbm, hbm, pl.BlockSpec(memory_space=pltpu.VMEM)),
         scratch_shapes=scratch,
@@ -508,6 +519,13 @@
             collective_id=0, has_side_effects=True, vmem_limit_bytes=56 * 1024 * 1024
         ),
     )(*arrays)
+    return pl.pallas_call(
+        hand_over,
+        out_shape=results,
+        in_specs=[hbm] * 4,
+        out_specs=(hbm,) * 4,
+        scratch_shapes=[vmem(r.shape, r.dtype) for r in results] + [dma((4,)), dma((4,))],
+    )(*made)
 
 
 def solution(mesh):

time: 71.6 us -> 62.4 us (0.87)
  local copies, waits for them, and re-layouts: 6.69 us -> 0 us
  Pallas kernels: 63.4 us -> 60.9 us
    unnamed x4 -> x0, local copies, waits for them, and re-layouts: 6.69 us -> none
    pallas_call x1 -> x2, Pallas kernels: 63.4 us -> 60.9 us  [the longest x1 58.8 us: per_device(): pl.pallas_call(functools.partial(kernel, dims), out_shape=results, in_spe...]
where the time goes in v2:
time: 62.4 us; the launch traced here: 62.2 us
  Pallas kernels  60.9 us (98%)
  between operations  1.29 us (2%)
    pallas_call x1, Pallas kernels, per_device(): pl.pallas_call(functools.partial(kernel, dims), out_shape=results, in_spe...  58.8 us
    pallas_call x1, Pallas kernels, per_device(): pl.pallas_call(hand_over, out_shape=results, in_specs=[hbm] * 4, out_spec...  2.13 us

profile of v2, /device:TPU:1, one launch (start us, length us, event | category | flops | bytes accessed | tf_op | source)
XLA Modules:
  0.0 62.2 jit_solution(1727385469282090998)
XLA Ops:
  1.3 58.8 %shard_map.120 = (bf16[128,2560]{1,0:T(8,128)(2,1)}, bf16[128,512]{1,0:T(8,128)(2,1)}, bf16[128,512]{1,0:T(8,128)(2,1)}, bf16[16,5120]{1,0:T(8,128)(2,1)}) custom-call(bf16[16,5120]{1,0:T(8,128)(2,1)} %prompt_rows.1, bf16[5120,512]{1,0:T(8,128)(2,1)} %key_weight.1, bf16[5120,512]{1,0:T(8,128)(2,1)} %value_weight.1, bf16[128,2560]{1,0:T(8,128)(2,1)} %queries.1, ...), custom_call_target="tpu_custom_call" | custom-call | tf_op jit(solution)/shard_map/pallas_call | solution.py:512
  60.1 2.1 %shard_map.121 = (bf16[128,2560]{1,0:T(8,128)(2,1)}, bf16[128,512]{1,0:T(8,128)(2,1)}, bf16[128,512]{1,0:T(8,128)(2,1)}, bf16[16,5120]{1,0:T(8,128)(2,1)}) custom-call(bf16[128,2560]{1,0:T(8,128)(2,1)} %get-tuple-element.8.refs_0_, bf16[128,512]{1,0:T(8,128)(2,1)} %get-tuple-element.9.refs_1_, bf16[128,512]{1,0:T(8,128)(2,1)} %get-tuple-element.10.refs_2_, ...), custom_call_target="tpu_custom_call" | custom-call | tf_op jit(solution)/shard_map/pallas_call | solution.py:522

commit v3 on v2

v3 whole, which is shorter than its diff:
```python
import functools

import jax
import jax.numpy as jnp
from jax import lax
from jax.experimental import pallas as pl
from jax.experimental.pallas import tpu as pltpu
from jax.sharding import PartitionSpec as P

MESH = pl.DeviceIdType.MESH
E = 128
KVH = 4
G = 2
GROUP = 5
ROWS = 128
HALF = 16
SCALE = E ** (-0.5)
LOG2E = 1.4426950408889634
RING = (((0, 1), (2, 0)), ((1, 2), (0, 2)))


def kernel(
    dims,
    prompt_rows,
    key_weight,
    value_weight,
    queries,
    own_keys,
    own_values,
    out_grad,
    first_length,
    resp_prompt,
    query_grad,
    key_grad,
    value_grad,
    prompt_grad,
    wk,
    wv,
    rows,
    q_in,
    g_in,
    own_in,
    scal_out,
    scal_in,
    scal,
    stage,
    kv_00,
    kv_01,
    kv_10,
    kv_11,
    keys_ab,
    values_ab,
    q_ab,
    g_ab,
    probs,
    dprobs,
    probs_t,
    dscores_t,
    parts,
    contrib,
    recv1,
    acc1,
    recv2,
    share,
    final,
    dq_out,
    own_out,
    w_sem,
    in_sem,
    x_send,
    x_recv,
    plane_send,
    plane_recv,
    ring_send,
    ring_recv,
    out_sem,
):
    kv = ((kv_00, kv_01), (kv_10, kv_11))
    n = dims[0]
    prompts = n
    plen = n * n * 2 * HALF
    depth = key_weight.shape[0]
    kcols = G * E
    qcols = G * GROUP * E
    r_index = lax.axis_index("resp")
    core = lax.rem(r_index, 2)
    chip = lax.div(r_index, 2)
    place = (lax.axis_index("prompt"), lax.div(chip, n), lax.rem(chip, n))
    other = 1 - core
    even = core == 0
    turned = (place[1], place[2], place[0])
    me = tuple(jnp.where(even, a, b) for a, b in zip(place, turned))
    partner_me = tuple(jnp.where(even, b, a) for a, b in zip(place, turned))

    def device(coords):
        y = jnp.where(even, coords[0], coords[2])
        z = jnp.where(even, coords[1], coords[0])
        x = jnp.where(even, coords[2], coords[1])
        return (y, (z * n + x) * 2 + core)

    near = [[lax.rem(me[d] + off, n) for off in range(n)] for d in range(3)]

    def peer(*moves):
        coords = list(me)
        for dim, off in moves:
            coords[dim] = near[dim][off]
        return device(coords)

    partner = (place[0], chip * 2 + other)

    steps = 2
    span = depth // steps
    mine_k = pl.ds(pl.multiple_of(core * kcols, kcols), kcols)
    theirs_k = pl.ds(pl.multiple_of(other * kcols, kcols), kcols)
    mine_q = pl.ds(pl.multiple_of(core * qcols, E), qcols)
    theirs_q = pl.ds(pl.multiple_of(other * qcols, E), qcols)

    rows_copy = pltpu.make_async_copy(prompt_rows, rows, in_sem.at[0])
    rows_copy.start()
    w_copies = {}
    for t, (src, dst) in enumerate(((key_weight, wk), (value_weight, wv))):
        for s in range(steps):
            at = pl.ds(s * span, span)
            w_copies[t, s] = pltpu.make_async_copy(src.at[at], dst.at[at], w_sem.at[t, s])
            w_copies[t, s].start()
    local = [
        pltpu.make_async_copy(own_keys.at[:, mine_k], own_in.at[0, 0], in_sem.at[1]),
        pltpu.make_async_copy(own_values.at[:, mine_k], own_in.at[0, 1], in_sem.at[2]),
        pltpu.make_async_copy(queries.at[:, mine_q], q_in.at[0], in_sem.at[3]),
        pltpu.make_async_copy(out_grad.at[:, mine_q], g_in.at[0], in_sem.at[4]),
    ]
    for c in local:
        c.start()

    barrier = pltpu.get_barrier_semaphore()
    pl.semaphore_signal(barrier, inc=1, device_id=partner, device_id_type=MESH)
    greeted = [((d, off),) for d in range(3) for off in range(1, n)]
    greeted += [((d, i), (e, j)) for d in range(3) for e in range(d + 1, 3) for i in range(1, n) for j in range(1, n)]
    for moves in greeted:
        pl.semaphore_signal(barrier, inc=1, device_id=peer(*moves), device_id_type=MESH)

    l_mine = first_length[0]
    a_mine = resp_prompt[0, 0]
    b_mine = resp_prompt[0, 1]
    lane8 = lax.broadcasted_iota(jnp.int32, (8, 128), 1)
    scal_out[...] = jnp.where(lane8 == 0, l_mine, jnp.where(lane8 == 1, a_mine, b_mine))
    rows_copy.wait()
    for t, weight in ((0, wk), (1, wv)):
        total = jnp.zeros((HALF, KVH * E), jnp.float32)
        for s in range(steps):
            w_copies[t, s].wait()
            at = slice(s * span, (s + 1) * span)
            total = total + jnp.dot(rows[:, at], weight[at, :], preferred_element_type=jnp.float32)
        total = total.astype(jnp.bfloat16)
        for head in range(KVH):
            stage[head // G, head % G, t] = total[:, head * E : (head + 1) * E]
    for g in range(G):
        for t in range(2):
            kv[g][t][me[0], me[1], me[2], core] = stage[core, g, t]

    pl.semaphore_wait(barrier, len(greeted) + 1)

    def swap(src, dst, index):
        c = pltpu.make_async_remote_copy(
            src_ref=src, dst_ref=dst, send_sem=x_send.at[index], recv_sem=x_recv.at[index],
            device_id=partner, device_id_type=MESH,
        )
        c.start()
        return c

    kv_swaps = {
        (g, t): swap(
            stage.at[other, g, t], kv[g][t].at[partner_me[0], partner_me[1], partner_me[2], core], g * 2 + t
        )
        for g in range(G)
        for t in range(2)
    }
    scal_swap = swap(scal_out, scal_in, 4)
    q_swap = swap(queries.at[:, theirs_q], q_in.at[1], 5)
    g_swap = swap(out_grad.at[:, theirs_q], g_in.at[1], 6)
    own_swaps = [
        swap(own_keys.at[:, theirs_k], own_in.at[1, 0], 7),
        swap(own_values.at[:, theirs_k], own_in.at[1, 1], 8),
    ]

    def ring_of(name):
        return RING[name[0]][name[1]][name[2]]

    def plane_of(name):
        return [d for d in range(3) if d != ring_of(name)]

    def remote(src, dst, sems, to):
        return pltpu.make_async_remote_copy(
            src_ref=src, dst_ref=dst, send_sem=sems[0], recv_sem=sems[1], device_id=to, device_id_type=MESH
        )

    def plane_sems(phase, g, t):
        return plane_send.at[phase], plane_recv.at[phase, g * 2 + t]

    def ring_sems(phase, g, t):
        return ring_send.at[phase], ring_recv.at[phase, g * 2 + t]

    def plane_arrived(phase, g, t):
        remote(recv2.at[g, t], recv2.at[g, t], plane_sems(phase, g, t), partner).wait_recv()

    def ring_arrived(phase, g, t):
        remote(recv1.at[g, t], recv1.at[g, t], ring_sems(phase, g, t), partner).wait_recv()

    def gather_plane(name):
        g, t, h = name
        a, b = plane_of(name)
        block = kv[g][t].at[me[0], me[1], me[2], h]
        for i in range(n):
            for j in range(n):
                if i + j > 0:
                    remote(block, block, plane_sems(0, g, t), peer((a, i), (b, j))).start()

    def gather_ring(name):
        g, t, h = name
        c = ring_of(name)
        index = [me[d] if d == c else slice(None) for d in range(3)]
        block = kv[g][t].at[index[0], index[1], index[2], h]
        for off in range(1, n):
            remote(block, block, ring_sems(0, g, t), peer((c, off))).start()

    for g in range(G):
        for t in range(2):
            kv_swaps[g, t].wait_recv()
            for h in range(2):
                gather_plane((g, t, h))

    scal_swap.wait_recv()
    to_smem = pltpu.make_async_copy(scal_in, scal, in_sem.at[5])
    to_smem.start()
    to_smem.wait()
    first = (l_mine, scal[0, 0])
    prompt_a = (a_mine, scal[0, 1])
    prompt_b = (b_mine, scal[0, 2])
    for c in local:
        c.wait()
    for c in own_swaps:
        c.wait_recv()
    q_swap.wait_recv()
    g_swap.wait_recv()

    sub_j = lax.broadcasted_iota(jnp.int32, (ROWS, E), 0)
    lane_i = lax.broadcasted_iota(jnp.int32, (ROWS, E), 1)
    lane_1 = lax.broadcasted_iota(jnp.int32, (1, E), 1)
    half_1, half_2 = slice(0, E), slice(E, 2 * E)

    def prepare(g, d):
        in_a = jnp.where(sub_j < first[d], 1.0, 0.0).astype(jnp.bfloat16)
        in_b = jnp.where(sub_j < first[d], 0.0, 1.0).astype(jnp.bfloat16)
        for h in range(GROUP):
            cols = slice((g * GROUP + h) * E, (g * GROUP + h + 1) * E)
            at = slice(h * E, (h + 1) * E)
            for src, dst in ((q_in, q_ab), (g_in, g_ab)):
                value = src[d, :, cols]
                dst[g, d, at, half_1] = value * in_a
                dst[g, d, at, half_2] = value * in_b
        for t, dst in ((0, keys_ab), (1, values_ab)):
            for cols in (half_1, half_2):
                dst[g, d, plen:, cols] = own_in[d, t, :, g * E : (g + 1) * E]

    def fill(g, t, dst):
        def along(axis):
            for d in range(2):
                for cols, prompt in ((half_1, prompt_a[d]), (half_2, prompt_b[d])):
                    block = kv[g][t][prompt] if axis == 0 else kv[g][t][:, :, prompt]
                    dst[g, d, :plen, cols] = block.reshape(plen, E)

        pl.when(even)(lambda: along(0))
        pl.when(core == 1)(lambda: along(2))

    both = (((1,), (1,)), ((), ()))

    def probabilities(g, d):
        boundary = first[d]
        probs[d] = lax.dot_general(keys_ab[g, d], q_ab[g, d], both, preferred_element_type=jnp.float32)
        seen = (sub_j <= lane_i) & ((sub_j < boundary) == (lane_i < boundary))
        for h in range(GROUP):
            at = slice(h * E, (h + 1) * E)
            s_pre = probs[d, :plen, at]
            s_own = jnp.where(seen, probs[d, plen:, at], -jnp.inf)
            top = jnp.maximum(jnp.max(s_pre, axis=0, keepdims=True), jnp.max(s_own, axis=0, keepdims=True))
            e_pre = jnp.exp2((s_pre - top) * (SCALE * LOG2E))
            e_own = jnp.exp2((s_own - top) * (SCALE * LOG2E))
            total = jnp.sum(e_pre, axis=0, keepdims=True) + jnp.sum(e_own, axis=0, keepdims=True)
            inverse = 1.0 / total
            p_pre = e_pre * inverse
            p_own = e_own * inverse
            probs[d, :plen, at] = p_pre
            probs[d, plen:, at] = p_own
            probs_t[d, :plen, at] = p_pre.astype(jnp.bfloat16)
            probs_t[d, plen:, at] = p_own.astype(jnp.bfloat16)
        parts[d] = jnp.dot(probs_t[d], g_ab[g, d], preferred_element_type=jnp.float32)
        own_out[d, 1, :, g * E : (g + 1) * E] = (parts[d, plen:, half_1] + parts[d, plen:, half_2]).astype(jnp.bfloat16)

    def score_gradients(g, d):
        dprobs[...] = lax.dot_general(values_ab[g, d], g_ab[g, d], both, preferred_element_type=jnp.float32)
        for h in range(GROUP):
            at = slice(h * E, (h + 1) * E)
            dp = dprobs[:, at]
            delta = jnp.sum(probs_t[d, :, at].astype(jnp.float32) * dp, axis=0, keepdims=True)
            dscores_t[g, d, :, at] = (probs[d, :, at] * (dp - delta)).astype(jnp.bfloat16)
        parts[d] = jnp.dot(dscores_t[g, d], q_ab[g, d], preferred_element_type=jnp.float32)
        own_out[d, 0, :, g * E : (g + 1) * E] = (
            (parts[d, plen:, half_1] + parts[d, plen:, half_2]) * SCALE
        ).astype(jnp.bfloat16)

    def query_gradients(g, d):
        dq_t = jnp.dot(keys_ab[g, d].T, dscores_t[g, d], preferred_element_type=jnp.float32)
        for h in range(GROUP):
            at = slice(h * E, (h + 1) * E)
            picked = jnp.where(lane_1 < first[d], dq_t[:E, at], dq_t[E:, at]) * SCALE
            cols = slice((g * GROUP + h) * E, (g * GROUP + h + 1) * E)
            dq_out[d, :, cols] = picked.T.astype(jnp.bfloat16)

    def contribute(g, t):
        unit = SCALE if t == 0 else 1.0

        def along(axis):
            for p in range(prompts):
                total = None
                for d in range(2):
                    for cols, prompt in ((half_1, prompt_a[d]), (half_2, prompt_b[d])):
                        gate = jnp.where(prompt == p, unit, 0.0).astype(jnp.float32)
                        term = parts[d, :plen, cols] * gate
                        total = term if total is None else total + term
                block = total.astype(jnp.bfloat16).reshape(n, n, 2, HALF, E)
                if axis == 0:
                    contrib[g, t, p] = block
                else:
                    contrib[g, t, :, :, p] = block

        pl.when(even)(lambda: along(0))
        pl.when(core == 1)(lambda: along(2))

    def scatter_ring(name):
        g, t, h = name
        c = ring_of(name)
        for off in range(1, n):
            index = tuple(near[d][off] if d == c else slice(None) for d in range(3))
            remote(
                contrib.at[(g, t) + index + (h,)], recv1.at[g, t, h, off - 1], ring_sems(1, g, t), peer((c, off))
            ).start()

    def scatter_plane(name):
        g, t, h = name
        c = ring_of(name)
        index = tuple(me[d] if d == c else slice(None) for d in range(3))
        total = contrib[(g, t) + index + (h,)].astype(jnp.float32)
        for off in range(1, n):
            total = total + recv1[g, t, h, off - 1].astype(jnp.float32)
        acc1[g, t, h] = total.astype(jnp.bfloat16)
        a, b = plane_of(name)
        for i in range(n):
            for j in range(n):
                if i + j > 0:
                    remote(
                        acc1.at[g, t, h, near[a][i], near[b][j]], recv2.at[g, t, h, i * n + j - 1],
                        plane_sems(1, g, t), peer((a, i), (b, j)),
                    ).start()

    def scatter_end(name):
        g, t, h = name
        a, b = plane_of(name)
        total = acc1[g, t, h, me[a], me[b]].astype(jnp.float32)
        total = total + jnp.sum(recv2[g, t, h].astype(jnp.float32), axis=0)
        share[h, :, (t * G + g) * E : (t * G + g + 1) * E] = total.astype(jnp.bfloat16)

    for g in range(G):
        for d in range(2):
            prepare(g, d)
    for g in range(G):
        for t in range(2):
            plane_arrived(0, g, t)
            for h in range(2):
                gather_ring((g, t, h))

    for g in range(G):
        ring_arrived(0, g, 0)
        fill(g, 0, keys_ab)
        for d in range(2):
            probabilities(g, d)
        contribute(g, 1)
        for h in range(2):
            scatter_ring((g, 1, h))
        ring_arrived(0, g, 1)
        fill(g, 1, values_ab)
        for d in range(2):
            score_gradients(g, d)
        contribute(g, 0)
        for h in range(2):
            scatter_ring((g, 0, h))

    for g in range(G):
        for d in range(2):
            query_gradients(g, d)
    home = [
        pltpu.make_async_copy(dq_out.at[0], query_grad.at[:, mine_q], out_sem.at[0]),
        pltpu.make_async_copy(own_out.at[0, 0], key_grad.at[:, mine_k], out_sem.at[1]),
        pltpu.make_async_copy(own_out.at[0, 1], value_grad.at[:, mine_k], out_sem.at[2]),
    ]
    for c in home:
        c.start()
    away = [
        swap(dq_out.at[1], query_grad.at[:, mine_q], 9),
        swap(own_out.at[1, 0], key_grad.at[:, mine_k], 10),
        swap(own_out.at[1, 1], value_grad.at[:, mine_k], 11),
    ]

    backwards = [(g, t) for g in range(G) for t in (1, 0)]
    for g, t in backwards:
        ring_arrived(1, g, t)
        for h in range(2):
            scatter_plane((g, t, h))
    for g, t in backwards:
        plane_arrived(1, g, t)
        for h in range(2):
            scatter_end((g, t, h))

    final_swap = swap(share.at[other], final.at[core], 12)
    final[core] = share[core]
    final_swap.wait_recv()
    x_k = jnp.concatenate([final[0, :, :kcols], final[1, :, :kcols]], axis=1)
    x_v = jnp.concatenate([final[0, :, kcols:], final[1, :, kcols:]], axis=1)
    tile = 512
    for s in range(depth // tile):
        at = slice(s * tile, (s + 1) * tile)
        total = lax.dot_general(x_k, wk[at, :], both, preferred_element_type=jnp.float32)
        total = total + lax.dot_general(x_v, wv[at, :], both, preferred_element_type=jnp.float32)
        prompt_grad[:, at] = total.astype(jnp.bfloat16)

    for phase in range(2):
        remote(recv2, recv2, plane_sems(phase, 0, 0), partner).wait_send()
        remote(recv1, recv1, ring_sems(phase, 0, 0), partner).wait_send()
    for c in list(kv_swaps.values()) + own_swaps + away + [scal_swap, q_swap, g_swap, final_swap]:
        c.wait_send()
    for c in home:
        c.wait()
    for c in away:
        c.wait_recv()


def hand_over(*refs):
    sources, results, buffers, arrive, leave = refs[:4], refs[4:8], refs[8:12], refs[12], refs[13]
    inward = [pltpu.make_async_copy(a, b, arrive.at[i]) for i, (a, b) in enumerate(zip(sources, buffers))]
    outward = [pltpu.make_async_copy(b, c, leave.at[i]) for i, (b, c) in enumerate(zip(buffers, results))]
    for c in inward:
        c.start()
    for c, after in zip(inward, outward):
        c.wait()
        after.start()
    for c in outward:
        c.wait()


def per_device(dims, *arrays):
    ny, nz, nx = dims
    depth = arrays[0].shape[1]
    plen = nz * nx * 2 * HALF
    keys = plen + ROWS
    wide = GROUP * E
    bf16, f32 = jnp.bfloat16, jnp.float32
    assert ny == nz == nx
    n = nx
    vmem = pltpu.VMEM
    hbm = pl.BlockSpec(memory_space=pl.ANY)
    smem = pl.BlockSpec(memory_space=pltpu.SMEM)
    dma = pltpu.SemaphoreType.DMA
    scratch = [
        vmem((depth, KVH * E), bf16),
        vmem((depth, KVH * E), bf16),
        vmem((HALF, depth), bf16),
        vmem((2, ROWS, G * wide), bf16),
        vmem((2, ROWS, G * wide), bf16),
        vmem((2, 2, ROWS, G * E), bf16),
        vmem((8, 128), jnp.int32),
        vmem((8, 128), jnp.int32),
        pltpu.SMEM((8, 128), jnp.int32),
        vmem((2, G, 2, HALF, E), bf16),
    ]
    scratch += [vmem((n, n, n, 2, HALF, E), bf16)] * 4
    scratch += [
        vmem((G, 2, keys, 2 * E), bf16),
        vmem((G, 2, keys, 2 * E), bf16),
        vmem((G, 2, wide, 2 * E), bf16),
        vmem((G, 2, wide, 2 * E), bf16),
        vmem((2, keys, wide), f32),
        vmem((keys, wide), f32),
        vmem((2, keys, wide), bf16),
        vmem((G, 2, keys, wide), bf16),
        vmem((2, keys, 2 * E), f32),
        vmem((G, 2, n, n, n, 2, HALF, E), bf16),
        vmem((G, 2, 2, n - 1, n, n, HALF, E), bf16),
        vmem((G, 2, 2, n, n, HALF, E), bf16),
        vmem((G, 2, 2, n * n - 1, HALF, E), bf16),
        vmem((2, HALF, 2 * G * E), bf16),
        vmem((2, HALF, 2 * G * E), bf16),
        vmem((2, ROWS, G * wide), bf16),
        vmem((2, 2, ROWS, G * E), bf16),
        dma((2, 2)),
        dma((6,)),
        dma((13,)),
        dma((13,)),
        dma((2,)),
        dma((2, 2 * G)),
        dma((2,)),
        dma((2, 2 * G)),
        dma((3,)),
    ]
    shape = jax.ShapeDtypeStruct
    results = (
        shape((ROWS, KVH * wide), bf16),
        shape((ROWS, KVH * E), bf16),
        shape((ROWS, KVH * E), bf16),
        shape((HALF, depth), bf16),
    )
    made = pl.pallas_call(
        functools.partial(kernel, dims),
        out_shape=results,
        in_specs=[hbm] * 7 + [smem] * 2,
        out_specs=(hbm, hbm, hbm, pl.BlockSpec(memory_space=pltpu.VMEM)),
        scratch_shapes=scratch,
        compiler_params=pltpu.CompilerParams(
            collective_id=0, has_side_effects=True, vmem_limit_bytes=56 * 1024 * 1024
        ),
    )(*arrays)
    return pl.pallas_call(
        hand_over,
        out_shape=results,
        in_specs=[hbm] * 4,
        out_specs=(hbm,) * 4,
        scratch_shapes=[vmem(r.shape, r.dtype) for r in results] + [dma((4,)), dma((4,))],
    )(*made)


def solution(mesh):
    ny = mesh.shape["prompt"]
    chips = mesh.shape["resp"] // 2
    nx = round(chips**0.5)
    dims = (ny, chips // nx, nx)
    rows = P(("prompt", "resp"), None)
    return jax.shard_map(
        functools.partial(per_device, dims),
        mesh=mesh,
        in_specs=(rows, P(), P(), rows, rows, rows, rows, P(("prompt", "resp")), rows),
        out_specs=(rows, rows, rows, rows),
        check_vma=False,
    )
```

time: 62.4 us -> 53.8 us (0.86)
  Pallas kernels: 60.9 us -> 52.2 us
    pallas_call x1, Pallas kernels: 58.8 us -> 50.1 us  [per_device(): pl.pallas_call(functools.partial(kernel, dims), out_shape=results, in_spe...]
where the time goes in v3:
time: 53.8 us; the launch traced here: 53.7 us
  Pallas kernels  52.2 us (97%)
  between operations  1.45 us (3%)
    pallas_call x1, Pallas kernels, per_device(): pl.pallas_call(functools.partial(kernel, dims), out_shape=results, in_spe...  50.1 us
    pallas_call x1, Pallas kernels, per_device(): pl.pallas_call(hand_over, out_shape=results, in_specs=[hbm] * 4, out_spec...  2.13 us

profile of v3, /device:TPU:1, one launch (start us, length us, event | category | flops | bytes accessed | tf_op | source)
XLA Modules:
  0.0 53.7 jit_solution(15754186146998546446)
XLA Ops:
  1.3 50.1 %shard_map.120 = (bf16[128,2560]{1,0:T(8,128)(2,1)}, bf16[128,512]{1,0:T(8,128)(2,1)}, bf16[128,512]{1,0:T(8,128)(2,1)}, bf16[16,5120]{1,0:T(8,128)(2,1)}) custom-call(bf16[16,5120]{1,0:T(8,128)(2,1)} %prompt_rows.1, bf16[5120,512]{1,0:T(8,128)(2,1)} %key_weight.1, bf16[5120,512]{1,0:T(8,128)(2,1)} %value_weight.1, bf16[128,2560]{1,0:T(8,128)(2,1)} %queries.1, ...), custom_call_target="tpu_custom_call" | custom-call | tf_op jit(solution)/shard_map/pallas_call | solution.py:520
  51.4 2.1 %shard_map.121 = (bf16[128,2560]{1,0:T(8,128)(2,1)}, bf16[128,512]{1,0:T(8,128)(2,1)}, bf16[128,512]{1,0:T(8,128)(2,1)}, bf16[16,5120]{1,0:T(8,128)(2,1)}) custom-call(bf16[128,2560]{1,0:T(8,128)(2,1)} %get-tuple-element.8.refs_0_, bf16[128,512]{1,0:T(8,128)(2,1)} %get-tuple-element.9.refs_1_, bf16[128,512]{1,0:T(8,128)(2,1)} %get-tuple-element.10.refs_2_, ...), custom_call_target="tpu_custom_call" | custom-call | tf_op jit(solution)/shard_map/pallas_call | solution.py:530

commit v4 on v3

--- a/solution.py
+++ b/solution.py
@@ -16,7 +16,7 @@
 HALF = 16
 SCALE = E ** (-0.5)
 LOG2E = 1.4426950408889634
-RING = (((0, 1), (2, 0)), ((1, 2), (0, 2)))
+RING = ((0, 1), (2, 0))
 
 
 def kernel(
@@ -43,7 +43,10 @@
     scal_out,
     scal_in,
     scal,
+    scal_first,
+    scal_pair,
     stage,
+    planes,
     kv_00,
     kv_01,
     kv_10,
@@ -63,12 +66,17 @@
     recv2,
     share,
     final,
+    w_last,
+    prompt_sum,
+    prompt_out,
     dq_out,
     own_out,
     w_sem,
     in_sem,
     x_send,
     x_recv,
+    hop_send,
+    hop_recv,
     plane_send,
     plane_recv,
     ring_send,
@@ -92,19 +100,19 @@
     me = tuple(jnp.where(even, a, b) for a, b in zip(place, turned))
     partner_me = tuple(jnp.where(even, b, a) for a, b in zip(place, turned))
 
-    def device(coords):
-        y = jnp.where(even, coords[0], coords[2])
-        z = jnp.where(even, coords[1], coords[0])
-        x = jnp.where(even, coords[2], coords[1])
-        return (y, (z * n + x) * 2 + core)
-
     near = [[lax.rem(me[d] + off, n) for off in range(n)] for d in range(3)]
+    weight_y = (jnp.where(even, 1, 0), 0, jnp.where(even, 0, 1))
+    weight_r = (jnp.where(even, 0, 2 * n), jnp.where(even, 2 * n, 2), jnp.where(even, 2, 0))
+    add_y = [[near[d][off] * weight_y[d] for off in range(n)] for d in range(3)]
+    add_r = [[near[d][off] * weight_r[d] for off in range(n)] for d in range(3)]
 
     def peer(*moves):
-        coords = list(me)
-        for dim, off in moves:
-            coords[dim] = near[dim][off]
-        return device(coords)
+        off = [0, 0, 0]
+        for dim, by in moves:
+            off[dim] = by
+        y = add_y[0][off[0]] + add_y[2][off[2]]
+        r = add_r[0][off[0]] + add_r[1][off[1]] + add_r[2][off[2]] + core
+        return (y, r)
 
     partner = (place[0], chip * 2 + other)
 
@@ -129,8 +137,6 @@
         pltpu.make_async_copy(queries.at[:, mine_q], q_in.at[0], in_sem.at[3]),
         pltpu.make_async_copy(out_grad.at[:, mine_q], g_in.at[0], in_sem.at[4]),
     ]
-    for c in local:
-        c.start()
 
     barrier = pltpu.get_barrier_semaphore()
     pl.semaphore_signal(barrier, inc=1, device_id=partner, device_id_type=MESH)
@@ -138,10 +144,18 @@
     greeted += [((d, i), (e, j)) for d in range(3) for e in range(d + 1, 3) for i in range(1, n) for j in range(1, n)]
     for moves in greeted:
         pl.semaphore_signal(barrier, inc=1, device_id=peer(*moves), device_id_type=MESH)
-
-    l_mine = first_length[0]
-    a_mine = resp_prompt[0, 0]
-    b_mine = resp_prompt[0, 1]
+    scal_copies = [
+        pltpu.make_async_copy(first_length, scal_first, in_sem.at[6]),
+        pltpu.make_async_copy(resp_prompt, scal_pair, in_sem.at[7]),
+    ]
+    for c in scal_copies + local:
+        c.start()
+
+    for c in scal_copies:
+        c.wait()
+    l_mine = scal_first[0]
+    a_mine = scal_pair[0, 0]
+    b_mine = scal_pair[0, 1]
     lane8 = lax.broadcasted_iota(jnp.int32, (8, 128), 1)
     scal_out[...] = jnp.where(lane8 == 0, l_mine, jnp.where(lane8 == 1, a_mine, b_mine))
     rows_copy.wait()
@@ -154,9 +168,17 @@
         total = total.astype(jnp.bfloat16)
         for head in range(KVH):
             stage[head // G, head % G, t] = total[:, head * E : (head + 1) * E]
+
+    def plane_of(piece):
+        return [d for d in range(3) if d != RING[piece[0]][piece[1]]]
+
+    def plane_place(g, at):
+        zero, one = plane_of((g, 0)), plane_of((g, 1))
+        return tuple(jnp.where(even, at[i], at[j]) for i, j in zip(zero, one))
+
     for g in range(G):
-        for t in range(2):
-            kv[g][t][me[0], me[1], me[2], core] = stage[core, g, t]
+        a, b = plane_place(g, me)
+        planes[g, core, a, b] = stage[core, g]
 
     pl.semaphore_wait(barrier, len(greeted) + 1)
 
@@ -168,13 +190,53 @@
         c.start()
         return c
 
-    kv_swaps = {
-        (g, t): swap(
-            stage.at[other, g, t], kv[g][t].at[partner_me[0], partner_me[1], partner_me[2], core], g * 2 + t
+    kv_swaps = []
+    for g in range(G):
+        a, b = plane_place(g, partner_me)
+        kv_swaps.append(swap(stage.at[other, g], planes.at[g, core, a, b], g))
+
+    def remote(src, dst, sems, to):
+        return pltpu.make_async_remote_copy(
+            src_ref=src, dst_ref=dst, send_sem=sems[0], recv_sem=sems[1], device_id=to, device_id_type=MESH
         )
-        for g in range(G)
-        for t in range(2)
-    }
+
+    def hop_sems(g):
+        return hop_send.at[0], hop_recv.at[g]
+
+    def plane_sems(g, t):
+        return plane_send.at[0], plane_recv.at[g * 2 + t]
+
+    def ring_sems(phase, g, t):
+        return ring_send.at[phase], ring_recv.at[phase, g * 2 + t]
+
+    def hop_arrived(g):
+        remote(recv2.at[g], recv2.at[g], hop_sems(g), partner).wait_recv()
+
+    def plane_arrived(g, t):
+        remote(recv2.at[g, t], recv2.at[g, t], plane_sems(g, t), partner).wait_recv()
+
+    def ring_arrived(phase, g, t):
+        remote(recv1.at[g, t], recv1.at[g, t], ring_sems(phase, g, t), partner).wait_recv()
+
+    beyond = [(i, j) for i in range(n) for j in range(n) if i + j > 0]
+
+    def gather_plane(g):
+        for h in range(2):
+            a, b = plane_of((g, h))
+            block = planes.at[g, h, me[a], me[b]]
+            for i, j in beyond:
+                remote(block, block, hop_sems(g), peer((a, i), (b, j))).start()
+
+    def gather_ring(g, t, h):
+        c = RING[g][h]
+        index = tuple(me[d] if d == c else slice(None) for d in range(3)) + (h,)
+        for off in range(1, n):
+            remote(planes.at[g, h, :, :, t], kv[g][t].at[index], ring_sems(0, g, t), peer((c, off))).start()
+        kv[g][t][index] = planes[g, h, :, :, t]
+
+    for g in range(G):
+        kv_swaps[g].wait_recv()
+        gather_plane(g)
     scal_swap = swap(scal_out, scal_in, 4)
     q_swap = swap(queries.at[:, theirs_q], q_in.at[1], 5)
     g_swap = swap(out_grad.at[:, theirs_q], g_in.at[1], 6)
@@ -182,53 +244,6 @@
         swap(own_keys.at[:, theirs_k], own_in.at[1, 0], 7),
         swap(own_values.at[:, theirs_k], own_in.at[1, 1], 8),
     ]
-
-    def ring_of(name):
-        return RING[name[0]][name[1]][name[2]]
-
-    def plane_of(name):
-        return [d for d in range(3) if d != ring_of(name)]
-
-    def remote(src, dst, sems, to):
-        return pltpu.make_async_remote_copy(
-            src_ref=src, dst_ref=dst, send_sem=sems[0], recv_sem=sems[1], device_id=to, device_id_type=MESH
-        )
-
-    def plane_sems(phase, g, t):
-        return plane_send.at[phase], plane_recv.at[phase, g * 2 + t]
-
-    def ring_sems(phase, g, t):
-        return ring_send.at[phase], ring_recv.at[phase, g * 2 + t]
-
-    def plane_arrived(phase, g, t):
-        remote(recv2.at[g, t], recv2.at[g, t], plane_sems(phase, g, t), partner).wait_recv()
-
-    def ring_arrived(phase, g, t):
-        remote(recv1.at[g, t], recv1.at[g, t], ring_sems(phase, g, t), partner).wait_recv()
-
-    def gather_plane(name):
-        g, t, h = name
-        a, b = plane_of(name)
-        block = kv[g][t].at[me[0], me[1], me[2], h]
-        for i in range(n):
-            for j in range(n):
-                if i + j > 0:
-                    remote(block, block, plane_sems(0, g, t), peer((a, i), (b, j))).start()
-
-    def gather_ring(name):
-        g, t, h = name
-        c = ring_of(name)
-        index = [me[d] if d == c else slice(None) for d in range(3)]
-        block = kv[g][t].at[index[0], index[1], index[2], h]
-        for off in range(1, n):
-            remote(block, block, ring_sems(0, g, t), peer((c, off))).start()
-
-    for g in range(G):
-        for t in range(2):
-            kv_swaps[g, t].wait_recv()
-            for h in range(2):
-                gather_plane((g, t, h))
-
     scal_swap.wait_recv()
     to_smem = pltpu.make_async_copy(scal_in, scal, in_sem.at[5])
     to_smem.start()
@@ -274,9 +289,11 @@
 
     both = (((1,), (1,)), ((), ()))
 
+    def scores(g, d):
+        probs[d] = lax.dot_general(keys_ab[g, d], q_ab[g, d], both, preferred_element_type=jnp.float32)
+
     def probabilities(g, d):
         boundary = first[d]
-        probs[d] = lax.dot_general(keys_ab[g, d], q_ab[g, d], both, preferred_element_type=jnp.float32)
         seen = (sub_j <= lane_i) & ((sub_j < boundary) == (lane_i < boundary))
         for h in range(GROUP):
             at = slice(h * E, (h + 1) * E)
@@ -296,11 +313,13 @@
         parts[d] = jnp.dot(probs_t[d], g_ab[g, d], preferred_element_type=jnp.float32)
         own_out[d, 1, :, g * E : (g + 1) * E] = (parts[d, plen:, half_1] + parts[d, plen:, half_2]).astype(jnp.bfloat16)
 
+    def prob_gradients(g, d):
+        dprobs[d] = lax.dot_general(values_ab[g, d], g_ab[g, d], both, preferred_element_type=jnp.float32)
+
     def score_gradients(g, d):
-        dprobs[...] = lax.dot_general(values_ab[g, d], g_ab[g, d], both, preferred_element_type=jnp.float32)
         for h in range(GROUP):
             at = slice(h * E, (h + 1) * E)
-            dp = dprobs[:, at]
+            dp = dprobs[d, :, at]
             delta = jnp.sum(probs_t[d, :, at].astype(jnp.float32) * dp, axis=0, keepdims=True)
             dscores_t[g, d, :, at] = (probs[d, :, at] * (dp - delta)).astype(jnp.bfloat16)
         parts[d] = jnp.dot(dscores_t[g, d], q_ab[g, d], preferred_element_type=jnp.float32)
@@ -336,67 +355,78 @@
         pl.when(even)(lambda: along(0))
         pl.when(core == 1)(lambda: along(2))
 
-    def scatter_ring(name):
-        g, t, h = name
-        c = ring_of(name)
+    def scatter_ring(g, t, h):
+        c = RING[g][h]
         for off in range(1, n):
             index = tuple(near[d][off] if d == c else slice(None) for d in range(3))
             remote(
                 contrib.at[(g, t) + index + (h,)], recv1.at[g, t, h, off - 1], ring_sems(1, g, t), peer((c, off))
             ).start()
 
-    def scatter_plane(name):
-        g, t, h = name
-        c = ring_of(name)
-        index = tuple(me[d] if d == c else slice(None) for d in range(3))
-        total = contrib[(g, t) + index + (h,)].astype(jnp.float32)
-        for off in range(1, n):
-            total = total + recv1[g, t, h, off - 1].astype(jnp.float32)
-        acc1[g, t, h] = total.astype(jnp.bfloat16)
-        a, b = plane_of(name)
-        for i in range(n):
-            for j in range(n):
-                if i + j > 0:
-                    remote(
-                        acc1.at[g, t, h, near[a][i], near[b][j]], recv2.at[g, t, h, i * n + j - 1],
-                        plane_sems(1, g, t), peer((a, i), (b, j)),
-                    ).start()
-
-    def scatter_end(name):
-        g, t, h = name
-        a, b = plane_of(name)
-        total = acc1[g, t, h, me[a], me[b]].astype(jnp.float32)
-        total = total + jnp.sum(recv2[g, t, h].astype(jnp.float32), axis=0)
-        share[h, :, (t * G + g) * E : (t * G + g + 1) * E] = total.astype(jnp.bfloat16)
+    def scatter_plane(g, t):
+        ring_arrived(1, g, t)
+        for h in range(2):
+            c = RING[g][h]
+            index = tuple(me[d] if d == c else slice(None) for d in range(3))
+            total = contrib[(g, t) + index + (h,)].astype(jnp.float32)
+            for off in range(1, n):
+                total = total + recv1[g, t, h, off - 1].astype(jnp.float32)
+            acc1[g, t, h] = total.astype(jnp.bfloat16)
+            a, b = plane_of((g, h))
+            for i, j in beyond:
+                remote(
+                    acc1.at[g, t, h, near[a][i], near[b][j]], recv2.at[g, t, h, i * n + j - 1], plane_sems(g, t),
+                    peer((a, i), (b, j)),
+                ).start()
+
+    def scatter_end(g, t):
+        plane_arrived(g, t)
+        for h in range(2):
+            a, b = plane_of((g, h))
+            total = acc1[g, t, h, me[a], me[b]].astype(jnp.float32)
+            total = total + jnp.sum(recv2[g, t, h].astype(jnp.float32), axis=0)
+            share[g, t, h] = total.astype(jnp.bfloat16)
+        c = swap(share.at[g, t, other], final.at[g, t, core], 12 + g * 2 + t)
+        final[g, t, core] = share[g, t, core]
+        return c
 
     for g in range(G):
         for d in range(2):
             prepare(g, d)
     for g in range(G):
+        hop_arrived(g)
         for t in range(2):
-            plane_arrived(0, g, t)
             for h in range(2):
-                gather_ring((g, t, h))
+                gather_ring(g, t, h)
 
     for g in range(G):
         ring_arrived(0, g, 0)
         fill(g, 0, keys_ab)
         for d in range(2):
+            scores(g, d)
+        for d in range(2):
             probabilities(g, d)
         contribute(g, 1)
         for h in range(2):
-            scatter_ring((g, 1, h))
+            scatter_ring(g, 1, h)
         ring_arrived(0, g, 1)
         fill(g, 1, values_ab)
+        for d in range(2):
+            prob_gradients(g, d)
         for d in range(2):
             score_gradients(g, d)
         contribute(g, 0)
         for h in range(2):
-            scatter_ring((g, 0, h))
-
-    for g in range(G):
-        for d in range(2):
-            query_gradients(g, d)
+            scatter_ring(g, 0, h)
+
+    for d in range(2):
+        query_gradients(0, d)
+    for t in (1, 0):
+        scatter_plane(0, t)
+    for d in range(2):
+        query_gradients(1, d)
+    for t in (1, 0):
+        scatter_plane(1, t)
     home = [
         pltpu.make_async_copy(dq_out.at[0], query_grad.at[:, mine_q], out_sem.at[0]),
         pltpu.make_async_copy(own_out.at[0, 0], key_grad.at[:, mine_k], out_sem.at[1]),
@@ -410,34 +440,52 @@
         swap(own_out.at[1, 1], value_grad.at[:, mine_k], 11),
     ]
 
-    backwards = [(g, t) for g in range(G) for t in (1, 0)]
-    for g, t in backwards:
-        ring_arrived(1, g, t)
-        for h in range(2):
-            scatter_plane((g, t, h))
-    for g, t in backwards:
-        plane_arrived(1, g, t)
-        for h in range(2):
-            scatter_end((g, t, h))
-
-    final_swap = swap(share.at[other], final.at[core], 12)
-    final[core] = share[core]
-    final_swap.wait_recv()
-    x_k = jnp.concatenate([final[0, :, :kcols], final[1, :, :kcols]], axis=1)
-    x_v = jnp.concatenate([final[0, :, kcols:], final[1, :, kcols:]], axis=1)
     tile = 512
-    for s in range(depth // tile):
-        at = slice(s * tile, (s + 1) * tile)
-        total = lax.dot_general(x_k, wk[at, :], both, preferred_element_type=jnp.float32)
-        total = total + lax.dot_general(x_v, wv[at, :], both, preferred_element_type=jnp.float32)
-        prompt_grad[:, at] = total.astype(jnp.bfloat16)
+    tiles = [slice(i * tile, (i + 1) * tile) for i in range(depth // tile)]
+
+    def last_product(g, t, at):
+        weight = (wk, wv)[t]
+        total = None
+        for c in range(2):
+            head = slice((c * G + g) * E, (c * G + g + 1) * E)
+            term = lax.dot_general(final[g, t, c], weight[at, head], both, preferred_element_type=jnp.float32)
+            total = term if total is None else total + term
+        return total
+
+    for c in range(2):
+        w_last[:, c * E : (c + 1) * E] = wk[:, (c * G + 1) * E : (c * G + 2) * E]
+
+    final_swaps = [scatter_end(0, 1), scatter_end(0, 0)]
+    for c in final_swaps:
+        c.wait_recv()
+    for at in tiles:
+        prompt_sum[:, at] = last_product(0, 1, at) + last_product(0, 0, at)
+    final_swaps.append(scatter_end(1, 1))
+    final_swaps[2].wait_recv()
+    for at in tiles:
+        prompt_sum[:, at] = prompt_sum[:, at] + last_product(1, 1, at)
+    final_swaps.append(scatter_end(1, 0))
+    final_swaps[3].wait_recv()
+    x_last = jnp.concatenate([final[1, 0, 0], final[1, 0, 1]], axis=1)
+    prompt_copies = []
+    parted = len(tiles) // 2
+    for k, group in enumerate((tiles[:parted], tiles[parted:])):
+        for at in group:
+            total = lax.dot_general(x_last, w_last[at, :], both, preferred_element_type=jnp.float32)
+            prompt_out[:, at] = (prompt_sum[:, at] + total).astype(jnp.bfloat16)
+        whole = slice(group[0].start, group[-1].stop)
+        prompt_copies.append(
+            pltpu.make_async_copy(prompt_out.at[:, whole], prompt_grad.at[:, whole], out_sem.at[3 + k])
+        )
+        prompt_copies[k].start()
 
     for phase in range(2):
-        remote(recv2, recv2, plane_sems(phase, 0, 0), partner).wait_send()
         remote(recv1, recv1, ring_sems(phase, 0, 0), partner).wait_send()
-    for c in list(kv_swaps.values()) + own_swaps + away + [scal_swap, q_swap, g_swap, final_swap]:
+    remote(recv2, recv2, hop_sems(0), partner).wait_send()
+    remote(recv2, recv2, plane_sems(0, 0), partner).wait_send()
+    for c in kv_swaps + own_swaps + away + [scal_swap, q_swap, g_swap] + final_swaps:
         c.wait_send()
-    for c in home:
+    for c in home + prompt_copies:
         c.wait()
     for c in away:
         c.wait_recv()
@@ -467,7 +515,6 @@
     n = nx
     vmem = pltpu.VMEM
     hbm = pl.BlockSpec(memory_space=pl.ANY)
-    smem = pl.BlockSpec(memory_space=pltpu.SMEM)
     dma = pltpu.SemaphoreType.DMA
     scratch = [
         vmem((depth, KVH * E), bf16),
@@ -479,7 +526,10 @@
         vmem((8, 128), jnp.int32),
         vmem((8, 128), jnp.int32),
         pltpu.SMEM((8, 128), jnp.int32),
+        pltpu.SMEM((1,), jnp.int32),
+        pltpu.SMEM((1, 2), jnp.int32),
         vmem((2, G, 2, HALF, E), bf16),
+        vmem((G, 2, n, n, 2, HALF, E), bf16),
     ]
     scratch += [vmem((n, n, n, 2, HALF, E), bf16)] * 4
     scratch += [
@@ -488,7 +538,7 @@
         vmem((G, 2, wide, 2 * E), bf16),
         vmem((G, 2, wide, 2 * E), bf16),
         vmem((2, keys, wide), f32),
-        vmem((keys, wide), f32),
+        vmem((2, keys, wide), f32),
         vmem((2, keys, wide), bf16),
         vmem((G, 2, keys, wide), bf16),
         vmem((2, keys, 2 * E), f32),
@@ -496,19 +546,24 @@
         vmem((G, 2, 2, n - 1, n, n, HALF, E), bf16),
         vmem((G, 2, 2, n, n, HALF, E), bf16),
         vmem((G, 2, 2, n * n - 1, HALF, E), bf16),
-        vmem((2, HALF, 2 * G * E), bf16),
-        vmem((2, HALF, 2 * G * E), bf16),
+        vmem((G, 2, 2, HALF, E), bf16),
+        vmem((G, 2, 2, HALF, E), bf16),
+        vmem((depth, 2 * E), bf16),
+        vmem((HALF, depth), f32),
+        vmem((HALF, depth), bf16),
         vmem((2, ROWS, G * wide), bf16),
         vmem((2, 2, ROWS, G * E), bf16),
         dma((2, 2)),
-        dma((6,)),
-        dma((13,)),
-        dma((13,)),
+        dma((8,)),
+        dma((16,)),
+        dma((16,)),
+        dma((1,)),
+        dma((G,)),
+        dma((1,)),
+        dma((2 * G,)),
         dma((2,)),
         dma((2, 2 * G)),
-        dma((2,)),
-        dma((2, 2 * G)),
-        dma((3,)),
+        dma((5,)),
     ]
     shape = jax.ShapeDtypeStruct
     results = (
@@ -520,8 +575,8 @@
     made = pl.pallas_call(
         functools.partial(kernel, dims),
         out_shape=results,
-        in_specs=[hbm] * 7 + [smem] * 2,
-        out_specs=(hbm, hbm, hbm, pl.BlockSpec(memory_space=pltpu.VMEM)),
+        in_specs=[hbm] * 9,
+        out_specs=(hbm,) * 4,
         scratch_shapes=scratch,
         compiler_params=pltpu.CompilerParams(
             collective_id=0, has_side_effects=True, vmem_limit_bytes=56 * 1024 * 1024

time: 53.8 us -> 54 us (level)
  no operation moved by 1% of the time
where the time goes in v4:
time: 54 us; the launch traced here: 53.8 us
  Pallas kernels  52.4 us (97%)
  between operations  1.45 us (3%)
    pallas_call x1, Pallas kernels, per_device(): pl.pallas_call(functools.partial(kernel, dims), out_shape=results, in_spe...  50.3 us
    pallas_call x1, Pallas kernels, per_device(): pl.pallas_call(hand_over, out_shape=results, in_specs=[hbm] * 4, out_spec...  2.13 us

profile of v4, /device:TPU:1, one launch (start us, length us, event | category | flops | bytes accessed | tf_op | source)
XLA Modules:
  0.0 53.8 jit_solution(17569335935396476232)
XLA Ops:
  1.3 50.3 %shard_map.120 = (bf16[128,2560]{1,0:T(8,128)(2,1)}, bf16[128,512]{1,0:T(8,128)(2,1)}, bf16[128,512]{1,0:T(8,128)(2,1)}, bf16[16,5120]{1,0:T(8,128)(2,1)}) custom-call(bf16[16,5120]{1,0:T(8,128)(2,1)} %prompt_rows.1, bf16[5120,512]{1,0:T(8,128)(2,1)} %key_weight.1, bf16[5120,512]{1,0:T(8,128)(2,1)} %value_weight.1, bf16[128,2560]{1,0:T(8,128)(2,1)} %queries.1, ...), custom_call_target="tpu_custom_call" | custom-call | tf_op jit(solution)/shard_map/pallas_call | solution.py:575
  51.5 2.1 %shard_map.121 = (bf16[128,2560]{1,0:T(8,128)(2,1)}, bf16[128,512]{1,0:T(8,128)(2,1)}, bf16[128,512]{1,0:T(8,128)(2,1)}, bf16[16,5120]{1,0:T(8,128)(2,1)}) custom-call(bf16[128,2560]{1,0:T(8,128)(2,1)} %get-tuple-element.8.refs_0_, bf16[128,512]{1,0:T(8,128)(2,1)} %get-tuple-element.9.refs_1_, bf16[128,512]{1,0:T(8,128)(2,1)} %get-tuple-element.10.refs_2_, ...), custom_call_target="tpu_custom_call" | custom-call | tf_op jit(solution)/shard_map/pallas_call | solution.py:585

commit v5 on v4

--- a/solution.py
+++ b/solution.py
@@ -16,7 +16,7 @@
 HALF = 16
 SCALE = E ** (-0.5)
 LOG2E = 1.4426950408889634
-RING = ((0, 1), (2, 0))
+RING = (((0, 1), (2, 0)), ((1, 2), (0, 2)))
 
 
 def kernel(
@@ -170,15 +170,16 @@
             stage[head // G, head % G, t] = total[:, head * E : (head + 1) * E]
 
     def plane_of(piece):
-        return [d for d in range(3) if d != RING[piece[0]][piece[1]]]
-
-    def plane_place(g, at):
-        zero, one = plane_of((g, 0)), plane_of((g, 1))
+        return [d for d in range(3) if d != RING[piece[0]][piece[1]][piece[2]]]
+
+    def plane_place(g, t, at):
+        zero, one = plane_of((g, t, 0)), plane_of((g, t, 1))
         return tuple(jnp.where(even, at[i], at[j]) for i, j in zip(zero, one))
 
-    for g in range(G):
-        a, b = plane_place(g, me)
-        planes[g, core, a, b] = stage[core, g]
+    heads = [(g, t) for g in range(G) for t in range(2)]
+    for g, t in heads:
+        a, b = plane_place(g, t, me)
+        planes[g, t, core, a, b] = stage[core, g, t]
 
     pl.semaphore_wait(barrier, len(greeted) + 1)
 
@@ -191,17 +192,17 @@
         return c
 
     kv_swaps = []
-    for g in range(G):
-        a, b = plane_place(g, partner_me)
-        kv_swaps.append(swap(stage.at[other, g], planes.at[g, core, a, b], g))
+    for g, t in heads:
+        a, b = plane_place(g, t, partner_me)
+        kv_swaps.append(swap(stage.at[other, g, t], planes.at[g, t, core, a, b], g * 2 + t))
 
     def remote(src, dst, sems, to):
         return pltpu.make_async_remote_copy(
             src_ref=src, dst_ref=dst, send_sem=sems[0], recv_sem=sems[1], device_id=to, device_id_type=MESH
         )
 
-    def hop_sems(g):
-        return hop_send.at[0], hop_recv.at[g]
+    def hop_sems(g, t):
+        return hop_send.at[0], hop_recv.at[g * 2 + t]
 
     def plane_sems(g, t):
         return plane_send.at[0], plane_recv.at[g * 2 + t]
@@ -209,8 +210,8 @@
     def ring_sems(phase, g, t):
         return ring_send.at[phase], ring_recv.at[phase, g * 2 + t]
 
-    def hop_arrived(g):
-        remote(recv2.at[g], recv2.at[g], hop_sems(g), partner).wait_recv()
+    def hop_arrived(g, t):
+        remote(recv2.at[g, t], recv2.at[g, t], hop_sems(g, t), partner).wait_recv()
 
     def plane_arrived(g, t):
         remote(recv2.at[g, t], recv2.at[g, t], plane_sems(g, t), partner).wait_recv()
@@ -220,23 +221,23 @@
 
     beyond = [(i, j) for i in range(n) for j in range(n) if i + j > 0]
 
-    def gather_plane(g):
+    def gather_plane(g, t):
         for h in range(2):
-            a, b = plane_of((g, h))
-            block = planes.at[g, h, me[a], me[b]]
+            a, b = plane_of((g, t, h))
+            block = planes.at[g, t, h, me[a], me[b]]
             for i, j in beyond:
-                remote(block, block, hop_sems(g), peer((a, i), (b, j))).start()
+                remote(block, block, hop_sems(g, t), peer((a, i), (b, j))).start()
 
     def gather_ring(g, t, h):
-        c = RING[g][h]
+        c = RING[g][t][h]
         index = tuple(me[d] if d == c else slice(None) for d in range(3)) + (h,)
         for off in range(1, n):
-            remote(planes.at[g, h, :, :, t], kv[g][t].at[index], ring_sems(0, g, t), peer((c, off))).start()
-        kv[g][t][index] = planes[g, h, :, :, t]
-
-    for g in range(G):
-        kv_swaps[g].wait_recv()
-        gather_plane(g)
+            remote(planes.at[g, t, h], kv[g][t].at[index], ring_sems(0, g, t), peer((c, off))).start()
+        kv[g][t][index] = planes[g, t, h]
+
+    for g, t in heads:
+        kv_swaps[g * 2 + t].wait_recv()
+        gather_plane(g, t)
     scal_swap = swap(scal_out, scal_in, 4)
     q_swap = swap(queries.at[:, theirs_q], q_in.at[1], 5)
     g_swap = swap(out_grad.at[:, theirs_q], g_in.at[1], 6)
@@ -356,7 +357,7 @@
         pl.when(core == 1)(lambda: along(2))
 
     def scatter_ring(g, t, h):
-        c = RING[g][h]
+        c = RING[g][t][h]
         for off in range(1, n):
             index = tuple(near[d][off] if d == c else slice(None) for d in range(3))
             remote(
@@ -366,13 +367,13 @@
     def scatter_plane(g, t):
         ring_arrived(1, g, t)
         for h in range(2):
-            c = RING[g][h]
+            c = RING[g][t][h]
             index = tuple(me[d] if d == c else slice(None) for d in range(3))
             total = contrib[(g, t) + index + (h,)].astype(jnp.float32)
             for off in range(1, n):
                 total = total + recv1[g, t, h, off - 1].astype(jnp.float32)
             acc1[g, t, h] = total.astype(jnp.bfloat16)
-            a, b = plane_of((g, h))
+            a, b = plane_of((g, t, h))
             for i, j in beyond:
                 remote(
                     acc1.at[g, t, h, near[a][i], near[b][j]], recv2.at[g, t, h, i * n + j - 1], plane_sems(g, t),
@@ -382,7 +383,7 @@
     def scatter_end(g, t):
         plane_arrived(g, t)
         for h in range(2):
-            a, b = plane_of((g, h))
+            a, b = plane_of((g, t, h))
             total = acc1[g, t, h, me[a], me[b]].astype(jnp.float32)
             total = total + jnp.sum(recv2[g, t, h].astype(jnp.float32), axis=0)
             share[g, t, h] = total.astype(jnp.bfloat16)
@@ -393,11 +394,10 @@
     for g in range(G):
         for d in range(2):
             prepare(g, d)
-    for g in range(G):
-        hop_arrived(g)
-        for t in range(2):
-            for h in range(2):
-                gather_ring(g, t, h)
+    for g, t in heads:
+        hop_arrived(g, t)
+        for h in range(2):
+            gather_ring(g, t, h)
 
     for g in range(G):
         ring_arrived(0, g, 0)
@@ -481,7 +481,7 @@
 
     for phase in range(2):
         remote(recv1, recv1, ring_sems(phase, 0, 0), partner).wait_send()
-    remote(recv2, recv2, hop_sems(0), partner).wait_send()
+    remote(recv2, recv2, hop_sems(0, 0), partner).wait_send()
     remote(recv2, recv2, plane_sems(0, 0), partner).wait_send()
     for c in kv_swaps + own_swaps + away + [scal_swap, q_swap, g_swap] + final_swaps:
         c.wait_send()
@@ -529,7 +529,7 @@
         pltpu.SMEM((1,), jnp.int32),
         pltpu.SMEM((1, 2), jnp.int32),
         vmem((2, G, 2, HALF, E), bf16),
-        vmem((G, 2, n, n, 2, HALF, E), bf16),
+        vmem((G, 2, 2, n, n, HALF, E), bf16),
     ]
     scratch += [vmem((n, n, n, 2, HALF, E), bf16)] * 4
     scratch += [
@@ -558,7 +558,7 @@
         dma((16,)),
         dma((16,)),
         dma((1,)),
-        dma((G,)),
+        dma((2 * G,)),
         dma((1,)),
         dma((2 * G,)),
         dma((2,)),

time: 54 us -> 52 us (0.963)
  Pallas kernels: 52.4 us -> 50.4 us
    pallas_call x1, Pallas kernels: 50.3 us -> 48.3 us  [per_device(): pl.pallas_call(functools.partial(kernel, dims), out_shape=results, in_spe...]
where the time goes in v5:
time: 52 us; the launch traced here: 51.9 us
  Pallas kernels  50.4 us (97%)
  between operations  1.45 us (3%)
    pallas_call x1, Pallas kernels, per_device(): pl.pallas_call(functools.partial(kernel, dims), out_shape=results, in_spe...  48.3 us
    pallas_call x1, Pallas kernels, per_device(): pl.pallas_call(hand_over, out_shape=results, in_specs=[hbm] * 4, out_spec...  2.13 us

profile of v5, /device:TPU:1, one launch (start us, length us, event | category | flops | bytes accessed | tf_op | source)
XLA Modules:
  0.0 51.9 jit_solution(9113716622895662179)
XLA Ops:
  1.3 48.3 %shard_map.120 = (bf16[128,2560]{1,0:T(8,128)(2,1)}, bf16[128,512]{1,0:T(8,128)(2,1)}, bf16[128,512]{1,0:T(8,128)(2,1)}, bf16[16,5120]{1,0:T(8,128)(2,1)}) custom-call(bf16[16,5120]{1,0:T(8,128)(2,1)} %prompt_rows.1, bf16[5120,512]{1,0:T(8,128)(2,1)} %key_weight.1, bf16[5120,512]{1,0:T(8,128)(2,1)} %value_weight.1, bf16[128,2560]{1,0:T(8,128)(2,1)} %queries.1, ...), custom_call_target="tpu_custom_call" | custom-call | tf_op jit(solution)/shard_map/pallas_call | solution.py:575
  49.6 2.1 %shard_map.121 = (bf16[128,2560]{1,0:T(8,128)(2,1)}, bf16[128,512]{1,0:T(8,128)(2,1)}, bf16[128,512]{1,0:T(8,128)(2,1)}, bf16[16,5120]{1,0:T(8,128)(2,1)}) custom-call(bf16[128,2560]{1,0:T(8,128)(2,1)} %get-tuple-element.8.refs_0_, bf16[128,512]{1,0:T(8,128)(2,1)} %get-tuple-element.9.refs_1_, bf16[128,512]{1,0:T(8,128)(2,1)} %get-tuple-element.10.refs_2_, ...), custom_call_target="tpu_custom_call" | custom-call | tf_op jit(solution)/shard_map/pallas_call | solution.py:585

commit v6 on v5

--- a/solution.py
+++ b/solution.py
@@ -419,10 +419,10 @@
         for h in range(2):
             scatter_ring(g, 0, h)
 
+    for t in (1, 0):
+        scatter_plane(0, t)
     for d in range(2):
         query_gradients(0, d)
-    for t in (1, 0):
-        scatter_plane(0, t)
     for d in range(2):
         query_gradients(1, d)
     for t in (1, 0):

time: 52 us -> 52 us (level)
  no operation moved by 1% of the time
where the time goes in v6:
time: 52 us; the launch traced here: 51.9 us
  Pallas kernels  50.4 us (97%)
  between operations  1.45 us (3%)
    pallas_call x1, Pallas kernels, per_device(): pl.pallas_call(functools.partial(kernel, dims), out_shape=results, in_spe...  48.3 us
    pallas_call x1, Pallas kernels, per_device(): pl.pallas_call(hand_over, out_shape=results, in_specs=[hbm] * 4, out_spec...  2.13 us

profile of v6, /device:TPU:1, one launch (start us, length us, event | category | flops | bytes accessed | tf_op | source)
XLA Modules:
  0.0 51.9 jit_solution(11273088149026009247)
XLA Ops:
  1.3 48.3 %shard_map.120 = (bf16[128,2560]{1,0:T(8,128)(2,1)}, bf16[128,512]{1,0:T(8,128)(2,1)}, bf16[128,512]{1,0:T(8,128)(2,1)}, bf16[16,5120]{1,0:T(8,128)(2,1)}) custom-call(bf16[16,5120]{1,0:T(8,128)(2,1)} %prompt_rows.1, bf16[5120,512]{1,0:T(8,128)(2,1)} %key_weight.1, bf16[5120,512]{1,0:T(8,128)(2,1)} %value_weight.1, bf16[128,2560]{1,0:T(8,128)(2,1)} %queries.1, ...), custom_call_target="tpu_custom_call" | custom-call | tf_op jit(solution)/shard_map/pallas_call | solution.py:575
  49.6 2.1 %shard_map.121 = (bf16[128,2560]{1,0:T(8,128)(2,1)}, bf16[128,512]{1,0:T(8,128)(2,1)}, bf16[128,512]{1,0:T(8,128)(2,1)}, bf16[16,5120]{1,0:T(8,128)(2,1)}) custom-call(bf16[128,2560]{1,0:T(8,128)(2,1)} %get-tuple-element.8.refs_0_, bf16[128,512]{1,0:T(8,128)(2,1)} %get-tuple-element.9.refs_1_, bf16[128,512]{1,0:T(8,128)(2,1)} %get-tuple-element.10.refs_2_, ...), custom_call_target="tpu_custom_call" | custom-call | tf_op jit(solution)/shard_map/pallas_call | solution.py:585
